TPU v7x, 128 devices: a whole 4x4x4 slice. The times are simulated.
128 devices in a mesh: dp: 32 (over y, z, core), expert: 4 (over x).
Axes of the slice: x: 4, y: 4, z: 4, core: 2. Of those that a mesh axis runs over, the one named last changes fastest.
Arguments:
- gradient: float32 [32, 576, 7168], P(None, 'dp', 'expert')
- momentum: float32 [32, 576, 7168], P(None, 'dp', 'expert')
- owner_table: int32 [32], replicated, may hold values from 0 to 31, as said below
- shape_class: int32 [32], replicated, may hold values from 0 to 1
Outputs:
- new_moment: float32 [32, 576, 7168], P(None, 'dp', 'expert')
- update_rows: bfloat16 [32, 576, 7168], P(None, 'dp', 'expert')
- owned_update: bfloat16 [32, 576, 7168], P('dp', None, 'expert')
Inputs may be any that keep to these rules, and one draw needn't show every extreme that they name: owner_table is a permutation: every dp index owns exactly one matrix.
All inputs are finite; a program needn't handle non-finite values.
Results may differ from a plain program's by a relative error of at most 0.012.
The roundings to bfloat16 on the way count: a program that leaves them out, or rounds other values in their place, can miss the bound.
Values may be sent and summed in bfloat16 or wider, within the bound.
A program may use at most 128 MiB of HBM per device.

v0:
```python
import math

import jax
import jax.numpy as jnp
from jax import lax
from jax.sharding import PartitionSpec as P

COLS = 7168
ROUTER_ROWS = 384
ITERS = 4


MU_RATE = 0.95
EPSILON = 1e-07
COEF_A = 3.4445
COEF_B = -4.775
COEF_C = 2.0315


def gram_of(current):
    local = jnp.dot(current, current.T, preferred_element_type=jnp.float32)
    full = lax.psum(local, "expert")
    return full.astype(jnp.bfloat16)


def orthogonalize(matrix):
    current = matrix
    result = None
    for turn_index in range(ITERS):
        gram = gram_of(current)
        square = jnp.dot(gram, gram, preferred_element_type=jnp.float32)
        poly = (COEF_B * gram.astype(jnp.float32) + COEF_C * square).astype(jnp.bfloat16)
        result = COEF_A * current.astype(jnp.float32) + jnp.dot(
            poly, current, preferred_element_type=jnp.float32
        )
        if turn_index + 1 < ITERS:
            current = result.astype(jnp.bfloat16)
    return (0.2 * math.sqrt(COLS) * result).astype(jnp.bfloat16)


def orthogonalize_items(received):
    blocks = [orthogonalize(received[0, 0])]
    return jnp.stack(blocks)[None]


def body(gradient, momentum, owner_table, shape_class):
    group_count = lax.axis_size("expert")
    dp_count = lax.axis_size("dp")
    mats_here, rows_here, columns = gradient.shape
    place = lax.axis_index("dp")
    row_ids = place * rows_here + jnp.arange(rows_here, dtype=jnp.int32)
    live = ((shape_class[:, None] == 0) | (row_ids[None, :] < ROUTER_ROWS)).astype(jnp.float32)[
        :, :, None
    ]
    masked_grad = gradient * live
    masked_moment = momentum * live
    whole_count = jnp.float32(mats_here * rows_here * dp_count * columns * group_count)
    total = lax.psum(jnp.sum(masked_grad * masked_grad), ("dp", "expert"))
    clip = jnp.minimum(jnp.float32(1.0), jnp.sqrt(whole_count / total))
    new_moment = MU_RATE * masked_moment + clip * masked_grad
    blended = clip * masked_grad + MU_RATE * new_moment
    norm_m = jnp.sqrt(lax.psum(jnp.sum(blended * blended, axis=(1, 2)), ("dp", "expert")))
    start = (blended / (norm_m + EPSILON)[:, None, None]).astype(jnp.bfloat16)
    selector = (owner_table[None, :] == jnp.arange(dp_count, dtype=jnp.int32)[:, None]).astype(
        jnp.bfloat16
    )
    outgoing = jnp.einsum(
        "em,mrc->erc", selector, start, preferred_element_type=jnp.float32
    ).astype(jnp.bfloat16)[:, None]
    mapped = orthogonalize_items(
        lax.all_to_all(outgoing, "dp", split_axis=0, concat_axis=2, tiled=True)
    )
    returned = lax.all_to_all(mapped, "dp", split_axis=2, concat_axis=0, tiled=True)
    update_rows = jnp.take(returned[:, 0], owner_table, axis=0)
    owned_update = mapped[:, 0]
    return (new_moment, update_rows, owned_update)


def solution(mesh):
    return jax.shard_map(
        body,
        mesh=mesh,
        in_specs=(P(None, "dp", "expert"), P(None, "dp", "expert"), P(), P()),
        out_specs=(P(None, "dp", "expert"), P(None, "dp", "expert"), P("dp", None, "expert")),
        check_vma=False,
    )
```

profile of v0, /device:TPU:1, one launch (start us, length us, event | category | flops | bytes accessed | tf_op | source)
XLA Modules:
  0.0 442.0 jit_solution(11716507564541768915)
XLA Ops:
  1.4 3.9 multiply_reduce_fusion.1
  5.3 68.7 %psum.42 = f32[]{:T(128)} all-reduce(f32[]{:T(128)} %multiply_reduce_fusion.1), channel_id=1, replica_groups=mesh['dp'=32,'expert'=4] {'dp','expert'}, use_global_device_ids=true, to_apply=%region_1.0 | all-reduce | flops 1 | bytes 8 | tf_op jit(solution)/shard_map/psum | solution.py:58
  74.8 6.9 %multiply_reduce_fusion = (f32[32]{0:T(128)S(1)}, f32[32,18,1792]{2,0,1:T(8,128)}) fusion(f32[32,18,1792]{2,0,1:T(8,128)} %param.4, f32[32,18]{0,1:T(8,128)S(1)} %or_convert_fusion, f32[]{:T(128)S(6)} %min_shard_map.3, f32[32,18,1792]{2,0,1:T(8,128)} %param.5), kind=kLoop, calls=%fused_computation.6 | loop fusion | flops 9289696 | bytes 12388740 | tf_op jit(solution)/shard_map/reduce_sum | solution.py:62
  81.6 62.6 %psum.43 = f32[32]{0:T(128)S(1)} all-reduce(f32[32]{0:T(128)S(1)} %get-tuple-element.9), channel_id=1, replica_groups=mesh['dp'=32,'expert'=4] {'dp','expert'}, use_global_device_ids=true, to_apply=%region_3.0 | all-reduce | flops 32 | bytes 256 | tf_op jit(solution)/shard_map/psum | solution.py:62
  144.2 4.5 %fusion = bf16[32,1,18,1792]{3,0,2,1:T(8,128)(2,1)S(1)} fusion(f32[32]{0:T(128)S(1)} %sqrt_add_fusion, f32[32,18,1792]{2,0,1:T(8,128)} %get-tuple-element.10, f32[32,18,1792]{2,0,1:T(8,128)} %param.4, f32[]{:T(128)S(6)} %min_shard_map.3, f32[32,18]{0,1:T(8,128)S(1)} %or_convert_fusion, s32[32]{0:T(128)S(1)} %copy-done.2), kind=kOutput, calls=%fused_computation.11 | convolution fusion | flops 73286656 | bytes 10324484 | tf_op jit(solution)/shard_map/em,mrc->erc/dot_general | solution.py:67
  149.8 40.6 %all_to_all.8 = bf16[32,1,18,1792]{3,2,1,0:T(8,128)(2,1)S(1)} all-to-all(bf16[32,1,18,1792]{3,2,1,0:T(8,128)(2,1)S(1)} %copy.9), channel_id=1, replica_groups=mesh['dp'=32,'expert'=4] {'dp'}, dimensions={0} | all-to-all | bytes 4128768 | tf_op jit(solution)/shard_map/all_to_all | solution.py:71
  192.4 4.0 fusion.29
  196.4 30.8 %all-reduce.4 = bf16[576,576]{1,0:T(8,128)(2,1)} all-reduce(f32[576,576]{1,0:T(8,128)S(1)} %fusion.29), channel_id=1, replica_groups=mesh['dp'=32,'expert'=4] {'expert'}, use_global_device_ids=true, to_apply=%region_4.0 | all-reduce | flops 331776 | bytes 1990656 | tf_op jit(solution)/shard_map/psum | solution.py:22
  227.2 5.7 %add_convert_fusion.2 = bf16[576,1792]{1,0:T(8,128)(2,1)} fusion(bf16[576,1792]{1,0:T(8,128)(2,1)S(1)} %copy-done.1, bf16[576,576]{1,0:T(8,128)(2,1)} %all-reduce.4), kind=kOutput, calls=%fused_computation.4 | convolution fusion | flops 1577078784 | bytes 4792320 | tf_op jit(solution)/shard_map/dot_general | solution.py:33
  232.9 4.0 fusion.30
  236.9 28.0 %all-reduce.5 = bf16[576,576]{1,0:T(8,128)(2,1)S(1)} all-reduce(f32[576,576]{1,0:T(8,128)S(1)} %fusion.30), channel_id=1, replica_groups=mesh['dp'=32,'expert'=4] {'expert'}, use_global_device_ids=true, to_apply=%region_5.0 | all-reduce | flops 331776 | bytes 1990656 | tf_op jit(solution)/shard_map/psum | solution.py:22
  264.9 6.1 %add_convert_fusion.1 = bf16[576,1792]{1,0:T(8,128)(2,1)} fusion(bf16[576,1792]{1,0:T(8,128)(2,1)} %add_convert_fusion.2, bf16[576,576]{1,0:T(8,128)(2,1)S(1)} %all-reduce.5), kind=kOutput, calls=%fused_computation.3 | convolution fusion | flops 1577078784 | bytes 4792320 | tf_op jit(solution)/shard_map/dot_general | solution.py:33
  271.0 4.0 fusion.31
  275.0 28.1 %all-reduce.6 = bf16[576,576]{1,0:T(8,128)(2,1)S(1)} all-reduce(f32[576,576]{1,0:T(8,128)S(1)} %fusion.31), channel_id=1, replica_groups=mesh['dp'=32,'expert'=4] {'expert'}, use_global_device_ids=true, to_apply=%region_6.0 | all-reduce | flops 331776 | bytes 1990656 | tf_op jit(solution)/shard_map/psum | solution.py:22
  303.1 6.1 %add_convert_fusion = bf16[576,1792]{1,0:T(8,128)(2,1)} fusion(bf16[576,1792]{1,0:T(8,128)(2,1)} %add_convert_fusion.1, bf16[576,576]{1,0:T(8,128)(2,1)S(1)} %all-reduce.6), kind=kOutput, calls=%fused_computation.2 | convolution fusion | flops 1577078784 | bytes 4792320 | tf_op jit(solution)/shard_map/dot_general | solution.py:33
  309.1 4.0 fusion.32
  313.1 27.1 %all-reduce.7 = bf16[576,576]{1,0:T(8,128)(2,1)S(1)} all-reduce(f32[576,576]{1,0:T(8,128)S(1)} %fusion.32), channel_id=1, replica_groups=mesh['dp'=32,'expert'=4] {'expert'}, use_global_device_ids=true, to_apply=%region_7.0 | all-reduce | flops 331776 | bytes 1990656 | tf_op jit(solution)/shard_map/psum | solution.py:22
  340.3 4.8 %multiply_convert_fusion = bf16[576,1792]{1,0:T(8,128)(2,1)S(1)} fusion(bf16[576,1792]{1,0:T(8,128)(2,1)} %add_convert_fusion, bf16[576,576]{1,0:T(8,128)(2,1)S(1)} %all-reduce.7), kind=kOutput, calls=%fused_computation.1 | convolution fusion | flops 1578110976 | bytes 4792320 | tf_op jit(solution)/shard_map/dot_general | solution.py:33
  345.0 5.1 %copy.14 = bf16[1,1,576,1792]{3,1,0,2:T(2,128)(2,1)} copy(bf16[1,1,576,1792]{3,2,1,0:T(8,128)(2,1)S(1)} %bitcast.33) | data formatting | bytes 4128768 | tf_op jit(solution)/shard_map/broadcast_in_dim;stack | solution.py:43
  350.7 13.2 %reduce.2 = bf16[576,1792]{1,0:T(8,128)(2,1)S(1)} reduce(bf16[576,1,1,1792]{3,2,1,0:T(2,128)(2,1)} %bitcast.32, bf16[]{:T(256)} %broadcast.104), dimensions={1,2}, to_apply=%bitcast.31.reduce_sub_computation | reduce | bytes 4128770
  365.6 22.0 %all-to-all-start.1 = ((bf16[32,2,16128]{2,1,0:T(2,128)(2,1)}), bf16[32,2,16128]{2,1,0:T(2,128)(2,1)S(1)}, u32[]{:S(2)}, u32[]{:S(2)}) async-start(bf16[32,2,16128]{2,1,0:T(2,128)(2,1)} %reshape.68), calls=%async_computation.1 | async-start | bytes 4128768 | tf_op jit(solution)/shard_map/all_to_all | solution.py:73
  387.6 27.9 %all-to-all-done.1 = bf16[32,2,16128]{2,1,0:T(2,128)(2,1)S(1)} async-done(((bf16[32,2,16128]{2,1,0:T(2,128)(2,1)}), bf16[32,2,16128]{2,1,0:T(2,128)(2,1)S(1)}, u32[]{:S(2)}, u32[]{:S(2)}) %all-to-all-start.1) | async-done | bytes 2064416 | tf_op jit(solution)/shard_map/all_to_all | solution.py:73
  415.5 6.6 %reshape.69 = bf16[576,1,1,1792]{3,2,1,0:T(2,128)(2,1)} reshape(bf16[32,2,16128]{2,1,0:T(2,128)(2,1)S(1)} %all-to-all-done.1) | data formatting | bytes 4128768
  422.1 13.1 %bitcast_reduce_fusion = bf16[576,1792]{1,0:T(8,128)(2,1)S(1)} fusion(bf16[576,1,1,1792]{3,2,1,0:T(2,128)(2,1)} %reshape.69), kind=kLoop, calls=%fused_computation.48 | loop fusion | bytes 4128768 | tf_op jit(solution)/shard_map/all_to_all | solution.py:73
  (21 shorter events, 13.0 us)
Async XLA Ops:
  74.7 69.4 %copy-start.2 = (s32[32]{0:T(128)S(1)}, s32[32]{0:T(128)}, u32[]{:S(2)}) copy-start(s32[32]{0:T(128)} %param.6) | copy-start | bytes 388
  196.4 30.8 %copy-start.1 = (bf16[576,1792]{1,0:T(8,128)(2,1)S(1)}, bf16[576,1792]{1,0:T(8,128)(2,1)}, u32[]{:S(2)}) copy-start(bf16[576,1792]{1,0:T(8,128)(2,1)} %squeeze.6) | copy-start | bytes 6193156
  345.0 5.1 %copy-start = (bf16[576,1792]{1,0:T(8,128)(2,1)}, bf16[576,1792]{1,0:T(8,128)(2,1)S(1)}, u32[]{:S(2)}) copy-start(bf16[576,1792]{1,0:T(8,128)(2,1)S(1)} %multiply_convert_fusion) | copy-start | bytes 6193156
  365.6 50.0 %all-to-all-start.1 = ((bf16[32,2,16128]{2,1,0:T(2,128)(2,1)}), bf16[32,2,16128]{2,1,0:T(2,128)(2,1)S(1)}, u32[]{:S(2)}, u32[]{:S(2)}) async-start(bf16[32,2,16128]{2,1,0:T(2,128)(2,1)} %reshape.68), calls=%async_computation.1 | async-start | bytes 4128768 | tf_op jit(solution)/shard_map/all_to_all | solution.py:73
where the time goes:
time: 443 us; the launch traced here: 442 us
  blocking collectives  286 us (65%)
  matrix products  42.9 us (10%)
  local copies, waits for them, and re-layouts  36.7 us (8%)
  waiting for transfers between devices  27.9 us (6%)
  other arithmetic  25.1 us (6%)
  starting transfers between devices  22 us (5%)
    psum x4, blocking collectives, gram_of(): full = lax.psum(local, 'expert')  114 us
    psum x1, blocking collectives, body(): total = lax.psum(jnp.sum(masked_grad * masked_grad), ('dp', 'expert'))  68.7 us
    psum x1, blocking collectives, body(): lax.psum(jnp.sum(blended * blended, axis=(1, 2)), ('dp', 'expert'))  62.6 us
    all_to_all x1, blocking collectives, body(): lax.all_to_all(outgoing, 'dp', split_axis=0, concat_axis=2, tiled=True)  40.6 us
    all_to_all x1, waiting for transfers between devices, body(): lax.all_to_all(mapped, 'dp', split_axis=2, concat_axis=0, tiled=True)  27.9 us
    dot_general x4, matrix products, orthogonalize(): jnp.dot(poly, current, preferred_element_type=jnp.float32)  22.5 us
    all_to_all x1, starting transfers between devices, body(): lax.all_to_all(mapped, 'dp', split_axis=2, concat_axis=0, tiled=True)  22 us
    dot_general x4, matrix products, gram_of(): local = jnp.dot(current, current.T, preferred_element_type=jnp.float32)  16 us
  transfers between devices with their start and end apart: 1, of which 1 were waited for; matrix products, arithmetic and copies ran while one was open for 0% of the time, Pallas kernels for 0%

commit v1 on v0

v1 whole, which is shorter than its diff:
```python
import functools
import math

import jax
import jax.numpy as jnp
from jax import lax
from jax.experimental import pallas as pl
from jax.experimental.pallas import tpu as pltpu
from jax.sharding import PartitionSpec as P

MESH = pl.DeviceIdType.MESH
F32, BF16 = jnp.float32, jnp.bfloat16
ROWS, COLS, MATS, RDEV, CDEV = 576, 7168, 32, 18, 1792
ROUTER_ROWS = 384
LOADS = 6
MU_RATE, EPSILON = 0.95, 1e-07
VMEM_LIMIT = 56 * 1024 * 1024


def place():
    dp = lax.axis_index("dp")
    return dp, lax.axis_index("expert"), dp // 8, (dp // 2) % 4, dp % 2


def shifted(y, z, c, j):
    return (((y + j // 8) % 4) * 4 + (z + (j // 2) % 4) % 4) * 2 + (c + j % 2) % 2


def gather_kernel(owner_s, cls_s, g_hbm, m_hbm, x_ref, nm_hbm,
                  g, m, nm, zs, perm, zmain, zlo, lor, ar1, ar2,
                  in_sem, out_sem, s1, r1, s2, r2, sm, rm, sl, rl):
    dp, ex, y, z, c = place()
    per = ROWS // LOADS
    loads = []
    for k in range(LOADS):
        rows = pl.ds(k * per, per)
        for n, (src, dst) in enumerate(((g_hbm, g), (m_hbm, m))):
            cp = pltpu.make_async_copy(src.at[rows], dst.at[rows], in_sem.at[n, k])
            cp.start()
            loads.append(cp)

    barrier = pltpu.get_barrier_semaphore()

    def greet(j, _):
        pl.semaphore_signal(barrier, inc=1, device_id=(shifted(y, z, c, j), ex), device_id_type=MESH)
        return _
    lax.fori_loop(1, 32, greet, 0)

    def greet_x(j, _):
        zz, xx = (z + j % 4) % 4, (ex + j // 4) % 4
        pl.semaphore_signal(barrier, inc=1, device_id=((y * 4 + zz) * 2 + c, xx), device_id_type=MESH)
        return _
    lax.fori_loop(4, 16, greet_x, 0)

    lane = lax.broadcasted_iota(jnp.int32, (8, ROWS), 1)
    owner_row = jnp.zeros((8, ROWS), jnp.int32)
    mat = lax.broadcasted_iota(jnp.int32, (MATS, 128), 0)
    cls = jnp.zeros((MATS, 128), F32)
    for i in range(MATS):
        owner_row = jnp.where(lane % MATS == i, owner_s[i], owner_row)
        cls = jnp.where(mat == i, cls_s[i].astype(F32), cls)
    wanted = owner_row * RDEV + lane // MATS
    for k in range(ROWS // 32):
        o = lax.broadcasted_iota(jnp.int32, (32, ROWS), 0) + 32 * k
        if k < 16:
            key = (o // 16) * RDEV + o % 16
        else:
            key = ((o - 512) // 2) * RDEV + 16 + o % 2
        perm[32 * k:32 * (k + 1), :] = (key == wanted[0:1]).astype(F32).astype(BF16)

    def live_at(r):
        return jnp.where(dp * RDEV + r < ROUTER_ROWS, 1.0, 1.0 - cls)

    def stats(r, acc):
        live = live_at(r)
        rows = pl.ds(pl.multiple_of(r * MATS, MATS), MATS)
        gg, gm, mm = acc
        for t in range(CDEV // 128):
            gv = g[rows, t * 128:(t + 1) * 128] * live
            mv = m[rows, t * 128:(t + 1) * 128] * live
            mv = mv * (MU_RATE * MU_RATE)
            gg, gm, mm = gg + gv * gv, gm + gv * mv, mm + mv * mv
        return gg, gm, mm

    zero = jnp.zeros((MATS, 128), F32)
    acc = (zero, zero, zero)
    for k in range(LOADS):
        loads[2 * k].wait()
        loads[2 * k + 1].wait()
        acc = lax.fori_loop(k * (RDEV // LOADS), (k + 1) * (RDEV // LOADS), stats, acc)
    sums = [jnp.sum(a, axis=1, keepdims=True) for a in acc]
    col = lax.broadcasted_iota(jnp.int32, (MATS, 128), 1)
    mine = jnp.where(col == 0, sums[0], jnp.where(col == 1, sums[1], jnp.where(col == 2, sums[2], 0.0)))

    pl.semaphore_wait(barrier, 31 + 12)

    i1, i2 = y * 2 + c, ex * 4 + z
    ar1[i1] = mine

    def first_of(j):
        return (y + j // 2) % 4, (c + j % 2) % 2

    def first(j):
        yy, cc = first_of(j)
        return pltpu.make_async_remote_copy(
            src_ref=ar1.at[i1], dst_ref=ar1.at[i1], send_sem=s1.at[j], recv_sem=r1.at[i1],
            device_id=((yy * 4 + z) * 2 + cc, ex), device_id_type=MESH)

    def got(buf, slot, sem):
        return pltpu.make_async_copy(buf.at[slot], buf.at[slot], sem.at[slot])

    for j in range(1, 8):
        first(j).start()
    for j in range(1, 8):
        yy, cc = first_of(j)
        got(ar1, yy * 2 + cc, r1).wait()
    ar2[i2] = jnp.sum(ar1[...], axis=0)

    def second_of(j):
        return (z + j % 4) % 4, (ex + j // 4) % 4

    def second(j):
        zz, xx = second_of(j)
        return pltpu.make_async_remote_copy(
            src_ref=ar2.at[i2], dst_ref=ar2.at[i2], send_sem=s2.at[j], recv_sem=r2.at[i2],
            device_id=((y * 4 + zz) * 2 + c, xx), device_id_type=MESH)

    for j in range(1, 16):
        second(j).start()
    for j in range(1, 16):
        zz, xx = second_of(j)
        got(ar2, xx * 4 + zz, r2).wait()
    tot = jnp.sum(ar2[...], axis=0)
    gg, gm, mm = tot[:, 0:1], tot[:, 1:2], tot[:, 2:3]
    total = jnp.sum(gg, axis=0, keepdims=True)
    clip = jnp.minimum(1.0, jnp.sqrt(float(MATS * ROWS * COLS) / total))
    rate = (1.0 + MU_RATE) * clip
    sq = jnp.where(clip > 0.0, rate * rate * gg + 2.0 * rate * gm, 0.0) + mm
    norm = jnp.sqrt(jnp.maximum(sq, 0.0))
    inv = jnp.broadcast_to(1.0 / (norm + EPSILON), (MATS, 128))
    clip = jnp.broadcast_to(clip, (MATS, 128))

    def blend(r, _):
        live = live_at(r)
        lc = live * clip
        lm = live * MU_RATE
        rows = pl.ds(pl.multiple_of(r * MATS, MATS), MATS)
        for t in range(CDEV // 128):
            cols = slice(t * 128, (t + 1) * 128)
            gv = g[rows, cols] * lc
            nv = m[rows, cols] * lm + gv
            nm[rows, cols] = nv
            zs[rows, cols] = ((gv + MU_RATE * nv) * inv).astype(BF16)
        return _
    lax.fori_loop(0, RDEV, blend, 0)

    save = pltpu.make_async_copy(nm, nm_hbm, out_sem)
    save.start()

    for t in range(CDEV // 256):
        cols = slice(t * 256, (t + 1) * 256)
        out = jnp.dot(perm[...], zs[:, cols], preferred_element_type=F32)
        zmain[:, cols] = out[:512].astype(BF16)
        zlo[:, :, cols] = out[512:].reshape(MATS, 2, 256).astype(BF16)

    def block(ref, i):
        return ref.at[pl.ds(pl.multiple_of(i * 16, 16), 16)]

    def main_copy(j):
        to = shifted(y, z, c, j)
        return pltpu.make_async_remote_copy(
            src_ref=block(zmain, to), dst_ref=block(x_ref, dp), send_sem=sm.at[j], recv_sem=rm.at[dp],
            device_id=(to, ex), device_id_type=MESH)

    def lo_copy(j):
        to = shifted(y, z, c, j)
        return pltpu.make_async_remote_copy(
            src_ref=zlo.at[to], dst_ref=lor.at[dp], send_sem=sl.at[j], recv_sem=rl.at[dp],
            device_id=(to, ex), device_id_type=MESH)

    def send(j, _):
        main_copy(j).start()
        lo_copy(j).start()
        return _
    lax.fori_loop(1, 32, send, 0)
    own = pl.ds(pl.multiple_of(dp * 16, 16), 16)
    x_ref[own, :] = zmain[own, :]
    lor[dp] = zlo[dp]

    def receive(j, _):
        frm = shifted(y, z, c, j)
        pltpu.make_async_copy(block(x_ref, frm), block(x_ref, frm), rm.at[frm]).wait()
        pltpu.make_async_copy(lor.at[frm], lor.at[frm], rl.at[frm]).wait()
        return _
    lax.fori_loop(1, 32, receive, 0)
    x_ref[512:, :] = lor[...].astype(F32).reshape(64, CDEV).astype(BF16)

    def sent(j, _):
        main_copy(j).wait_send()
        lo_copy(j).wait_send()
        return _
    lax.fori_loop(1, 32, sent, 0)
    for j in range(1, 8):
        first(j).wait_send()
    for j in range(1, 16):
        second(j).wait_send()
    save.wait()


def gather_rows(owner, cls, g, m):
    D = pltpu.SemaphoreType.DMA
    return pl.pallas_call(
        gather_kernel,
        out_shape=(jax.ShapeDtypeStruct((ROWS, CDEV), BF16), jax.ShapeDtypeStruct((ROWS, CDEV), F32)),
        in_specs=[pl.BlockSpec(memory_space=pltpu.SMEM)] * 2 + [pl.BlockSpec(memory_space=pl.ANY)] * 2,
        out_specs=(pl.BlockSpec(memory_space=pltpu.VMEM), pl.BlockSpec(memory_space=pl.ANY)),
        scratch_shapes=[
            pltpu.VMEM((ROWS, CDEV), F32), pltpu.VMEM((ROWS, CDEV), F32), pltpu.VMEM((ROWS, CDEV), F32),
            pltpu.VMEM((ROWS, CDEV), BF16), pltpu.VMEM((ROWS, ROWS), BF16),
            pltpu.VMEM((512, CDEV), BF16), pltpu.VMEM((MATS, 2, CDEV), BF16), pltpu.VMEM((MATS, 2, CDEV), BF16),
            pltpu.VMEM((8, MATS, 128), F32), pltpu.VMEM((16, MATS, 128), F32),
            D((2, LOADS)), D, D((8,)), D((8,)), D((16,)), D((16,)), D((32,)), D((32,)), D((32,)), D((32,)),
        ],
        compiler_params=pltpu.CompilerParams(collective_id=0, has_side_effects=True, vmem_limit_bytes=VMEM_LIMIT),
    )(owner, cls, g, m)


COEF_A, COEF_B, COEF_C, ITERS = 3.4445, -4.775, 2.0315, 4
SCALE = 0.2 * math.sqrt(COLS)
CHUNK = 256
QUARTER = 7
PANELS = [(r, t) for r in range(9) for t in range(r // 2 + 1)]


def dot(a, b):
    return jnp.dot(a, b, preferred_element_type=F32)


def dot_t(a, b):
    return lax.dot_general(a, b, (((1,), (1,)), ((), ())), preferred_element_type=F32)


def slot_key(o):
    return jnp.where(o < 512, (o // 16) * RDEV + o % 16, ((o - 512) // 2) * RDEV + 16 + o % 2)


def halving_places(ex, c):
    near = ex + 1 - 2 * (ex % 2)
    far = 3 - ex
    first = (1 - c) * near + c * far
    second = (1 - c) * far + c * near

    def part(x):
        h = (1 - c) * (((x + 1) // 2) % 2) + c * (x // 2)
        q = (1 - c) * (x // 2) + c * (x % 2)
        return h, q
    return first, second, part


def update_kernel(owner_s, x_ref, up_ref, own_ref,
                  part, got1, got2, full, gram, t_ref, coef, u, ulo, vmain, vlo, v, perm, order,
                  xs, xr, sm, rm, sl, rl):
    dp, ex, y, z, c = place()
    first, second, part_of = halving_places(ex, c)
    h, q = part_of(ex)
    h1, q1 = part_of(first)

    barrier = pltpu.get_barrier_semaphore()

    def greet(j, _):
        pl.semaphore_signal(barrier, inc=1, device_id=(shifted(y, z, c, j), ex), device_id_type=MESH)
        return _
    lax.fori_loop(1, 32, greet, 0)
    for other in (first, second):
        pl.semaphore_signal(barrier, inc=1, device_id=(dp, other), device_id_type=MESH)

    for lo, hi in ((0, 256), (256, 512), (512, 576)):
        block = dot_t(x_ref[lo:, :], x_ref[lo:hi, :])
        for n, (r, t) in enumerate(PANELS):
            if lo <= 128 * t < hi:
                w = min(128, hi - 128 * t)
                piece = block[64 * r - lo:64 * r - lo + 64, 128 * t - lo:128 * t - lo + w]
                if w < 128:
                    piece = jnp.concatenate([piece, jnp.zeros((64, 128 - w), F32)], axis=1)
                part[n] = piece
    for n in range(len(PANELS), 4 * QUARTER):
        part[n] = jnp.zeros((64, 128), F32)

    pl.semaphore_wait(barrier, 33)

    def panels(ref, hh, qq):
        return ref.at[pl.ds((2 * hh + qq) * QUARTER, QUARTER)]

    def exchange(src, dst, n, to):
        return pltpu.make_async_remote_copy(
            src_ref=src, dst_ref=dst, send_sem=xs.at[n], recv_sem=xr.at[n],
            device_id=(dp, to), device_id_type=MESH)

    a1 = exchange(panels(part, h1, 1 - q1), got1.at[0], 0, first)
    a2 = exchange(panels(part, h1, q1), got1.at[1], 1, first)
    a1.start()
    a2.start()
    a1.wait_recv()
    pass_on, keep = pl.ds((2 * h + 1 - q) * QUARTER, QUARTER), pl.ds((2 * h + q) * QUARTER, QUARTER)
    part[pass_on] = part[pass_on] + got1[0]
    b = exchange(panels(part, h, 1 - q), got2, 2, second)
    b.start()
    a2.wait_recv()
    kept = part[keep] + got1[1]
    part[keep] = kept
    b.wait_recv()
    full[keep] = part[keep] + got2[...]
    c1 = exchange(panels(full, h, q), panels(full, h, q), 3, second)
    c2 = exchange(panels(full, h, q), panels(full, h, q), 4, first)
    c1.start()
    c2.start()
    c1.wait_recv()
    c3 = exchange(panels(full, h, 1 - q), panels(full, h, 1 - q), 5, first)
    c3.start()

    mat = lax.broadcasted_iota(jnp.int32, (MATS, ROWS), 0)
    owner_col = jnp.zeros((MATS, ROWS), jnp.int32)
    for i in range(MATS):
        owner_col = jnp.where(mat == i, owner_s[i], owner_col)
    key = slot_key(lax.broadcasted_iota(jnp.int32, (MATS, ROWS), 1))
    for r in range(RDEV):
        rows = slice(MATS * r, MATS * (r + 1))
        perm[rows, :] = (owner_col * RDEV + r == key).astype(F32).astype(BF16)
        order[rows, :] = (mat + MATS * r == key).astype(F32).astype(BF16)

    c2.wait_recv()
    c3.wait_recv()

    for n, (r, t) in enumerate(PANELS):
        w = min(128, ROWS - 128 * t)
        piece = full[n]
        gram[64 * r:64 * r + 64, 128 * t:128 * t + w] = piece[:, :w]
        if t < r // 2:
            gram[128 * t:128 * t + 128, 64 * r:64 * r + 64] = piece.T

    for k in range(ITERS):
        a16 = gram[...].astype(BF16)
        b16 = (COEF_B * a16.astype(F32) + COEF_C * dot(a16, a16)).astype(BF16)
        coef[k] = b16
        if k + 1 < ITERS:
            low = (gram[...] - a16.astype(F32)).astype(BF16)
            t_ref[...] = COEF_A * gram[...] + (dot(a16, b16) + dot(low, b16))
            t16 = t_ref[...].astype(BF16)
            tlow = (t_ref[...] - t16.astype(F32)).astype(BF16)
            gram[...] = COEF_A * t_ref[...] + (dot(b16, t16) + dot(b16, tlow))

    def block(ref, i):
        return ref.at[pl.ds(pl.multiple_of(i * 16, 16), 16)]

    def main_copy(j):
        to = shifted(y, z, c, j)
        return pltpu.make_async_remote_copy(
            src_ref=block(u, to), dst_ref=block(vmain, dp), send_sem=sm.at[j], recv_sem=rm.at[dp],
            device_id=(to, ex), device_id_type=MESH)

    def lo_copy(j):
        to = shifted(y, z, c, j)
        return pltpu.make_async_remote_copy(
            src_ref=ulo.at[to], dst_ref=vlo.at[dp], send_sem=sl.at[j], recv_sem=rl.at[dp],
            device_id=(to, ex), device_id_type=MESH)

    for n in range(CDEV // CHUNK):
        cols = slice(n * CHUNK, (n + 1) * CHUNK)
        cur = x_ref[:, cols]
        for k in range(ITERS):
            out = COEF_A * cur.astype(F32) + dot(coef[k], cur)
            if k + 1 < ITERS:
                cur = out.astype(BF16)
        res = (SCALE * out).astype(BF16)
        u[:, cols] = res
        ulo[:, :, cols] = res[512:].astype(F32).reshape(MATS, 2, CHUNK).astype(BF16)

    def send(j, _):
        main_copy(j).start()
        lo_copy(j).start()
        return _
    lax.fori_loop(1, 32, send, 0)

    own = pl.ds(pl.multiple_of(dp * 16, 16), 16)
    vmain[own, :] = u[own, :]
    vlo[dp] = ulo[dp]

    for n in range(CDEV // CHUNK):
        cols = slice(n * CHUNK, (n + 1) * CHUNK)
        own_ref[:, cols] = dot(order[...], u[:, cols]).astype(BF16)

    def receive(j, _):
        frm = shifted(y, z, c, j)
        pltpu.make_async_copy(block(vmain, frm), block(vmain, frm), rm.at[frm]).wait()
        pltpu.make_async_copy(vlo.at[frm], vlo.at[frm], rl.at[frm]).wait()
        return _
    lax.fori_loop(1, 32, receive, 0)
    v[...] = vlo[...].astype(F32).reshape(64, CDEV).astype(BF16)
    for n in range(CDEV // CHUNK):
        cols = slice(n * CHUNK, (n + 1) * CHUNK)
        up_ref[:, cols] = (dot(perm[:, :512], vmain[:, cols]) + dot(perm[:, 512:], v[:, cols])).astype(BF16)

    def sent(j, _):
        main_copy(j).wait_send()
        lo_copy(j).wait_send()
        return _
    lax.fori_loop(1, 32, sent, 0)
    for cp in (a1, a2, b, c1, c2, c3):
        cp.wait_send()


def update_rows_of(owner, x):
    D = pltpu.SemaphoreType.DMA
    V = pltpu.VMEM
    return pl.pallas_call(
        update_kernel,
        out_shape=(jax.ShapeDtypeStruct((ROWS, CDEV), BF16),) * 2,
        in_specs=[pl.BlockSpec(memory_space=pltpu.SMEM), pl.BlockSpec(memory_space=pltpu.VMEM)],
        out_specs=(pl.BlockSpec(memory_space=pltpu.VMEM),) * 2,
        scratch_shapes=[
            V((4 * QUARTER, 64, 128), F32), V((2, QUARTER, 64, 128), F32), V((QUARTER, 64, 128), F32),
            V((4 * QUARTER, 64, 128), F32), V((ROWS, ROWS), F32), V((ROWS, ROWS), F32), V((ITERS, ROWS, ROWS), BF16),
            V((ROWS, CDEV), BF16), V((MATS, 2, CDEV), BF16), V((512, CDEV), BF16), V((MATS, 2, CDEV), BF16),
            V((64, CDEV), BF16), V((ROWS, ROWS), BF16), V((ROWS, ROWS), BF16),
            D((6,)), D((6,)), D((32,)), D((32,)), D((32,)), D((32,)),
        ],
        compiler_params=pltpu.CompilerParams(collective_id=1, has_side_effects=True, vmem_limit_bytes=VMEM_LIMIT),
    )(owner, x)


def body(gradient, momentum, owner_table, shape_class):
    g = jnp.transpose(gradient, (1, 0, 2)).reshape(ROWS, CDEV)
    m = jnp.transpose(momentum, (1, 0, 2)).reshape(ROWS, CDEV)
    x, nm = gather_rows(owner_table, shape_class, g, m)
    up, own = update_rows_of(owner_table, x)
    new_moment = jnp.transpose(nm.reshape(RDEV, MATS, CDEV), (1, 0, 2))
    update = jnp.transpose(up.reshape(RDEV, MATS, CDEV), (1, 0, 2))
    return new_moment, update, own[None]


def solution(mesh):
    return jax.shard_map(
        body,
        mesh=mesh,
        in_specs=(P(None, "dp", "expert"), P(None, "dp", "expert"), P(), P()),
        out_specs=(P(None, "dp", "expert"), P(None, "dp", "expert"), P("dp", None, "expert")),
        check_vma=False,
    )
```

time: 443 us -> 150 us (0.34)
  blocking collectives: 286 us -> 0 us
  Pallas kernels: 0 us -> 141 us
  matrix products: 42.9 us -> 0 us
  local copies, waits for them, and re-layouts: 36.7 us -> 8.29 us
  waiting for transfers between devices: 27.9 us -> 0 us
  other arithmetic: 25.1 us -> 0 us
  starting transfers between devices: 22 us -> 0 us
    psum x6 -> x0, blocking collectives: 245 us -> none  [the longest x4 114 us: gram_of(): full = lax.psum(local, 'expert')]
    pallas_call x0 -> x2, Pallas kernels: none -> 141 us  [the longest x1 85.1 us: update_rows_of(): pl.pallas_call(update_kernel, out_shape=(jax.ShapeDtypeStruct((ROWS, CDEV...]
    dot_general x9 -> x0, matrix products: 42.9 us -> none  [the longest x4 22.5 us: orthogonalize(): jnp.dot(poly, current, preferred_element_type=jnp.float32)]
    all_to_all x1 -> x0, blocking collectives: 40.6 us -> none  [body(): lax.all_to_all(outgoing, 'dp', split_axis=0, concat_axis=2, tiled=True)]
    all_to_all x1 -> x0, waiting for transfers between devices: 27.9 us -> none  [body(): lax.all_to_all(mapped, 'dp', split_axis=2, concat_axis=0, tiled=True)]
    all_to_all x1 -> x0, starting transfers between devices: 22 us -> none  [body(): lax.all_to_all(mapped, 'dp', split_axis=2, concat_axis=0, tiled=True)]
    unnamed x1 -> x0, other arithmetic: 13.2 us -> none
    all_to_all x1 -> x0, local copies, waits for them, and re-layouts: 13.1 us -> none  [body(): lax.all_to_all(mapped, 'dp', split_axis=2, concat_axis=0, tiled=True)]
  transfers between devices with their start and end apart: 1 -> 0, of which waited for: 1 -> 0; matrix products, arithmetic and copies ran while one was open for 0% -> 0% of each run, Pallas kernels for 0% -> 0%
where the time goes in v1:
time: 150 us
  Pallas kernels  141 us (94%)
  local copies, waits for them, and re-layouts  8.29 us (6%)
    pallas_call x1, Pallas kernels, update_rows_of(): pl.pallas_call(update_kernel, out_shape=(jax.ShapeDtypeStruct((ROWS, CDEV...  85.1 us
    pallas_call x1, Pallas kernels, gather_rows(): pl.pallas_call(gather_kernel, out_shape=(jax.ShapeDtypeStruct((ROWS, CDEV...  55.8 us
    unnamed x7, local copies, waits for them, and re-layouts  8.29 us

profile of v1, /device:TPU:1, one launch (start us, length us, event | category | flops | bytes accessed | tf_op | source)
XLA Modules:
  0.0 149.9 jit_solution(18174965735348297198)
XLA Ops:
  0.6 55.8 %shard_map.67 = (bf16[576,1792]{1,0:T(8,128)(2,1)}, f32[576,1792]{1,0:T(8,128)}) custom-call(s32[32]{0:T(128)} %owner_s.3, s32[32]{0:T(128)} %cls_s.1, f32[576,1792]{1,0:T(8,128)} %bitcast.13, f32[576,1792]{1,0:T(8,128)} %bitcast.14), custom_call_target="tpu_custom_call" | custom-call | tf_op jit(solution)/shard_map/pallas_call | solution.py:212
  56.5 85.1 %shard_map.68 = (bf16[576,1792]{1,0:T(8,128)(2,1)}, bf16[576,1792]{1,0:T(8,128)(2,1)}) custom-call(s32[32]{0:T(128)} %owner_s.3, bf16[576,1792]{1,0:T(8,128)(2,1)} %get-tuple-element.8.x_ref), custom_call_target="tpu_custom_call" | custom-call | tf_op jit(solution)/shard_map/pallas_call | solution.py:415
  141.6 0.0 copy-start.1
  141.6 4.7 %copy.10 = f32[32,18,1792]{2,0,1:T(8,128)} copy(f32[32,18,1792]{2,0,1:T(8,128)} %bitcast.15) | data formatting | bytes 8257536
  146.3 0.0 copy-done.1
  146.3 0.0 copy-start
  146.3 1.3 copy.11
  147.6 1.0 copy-done
  148.6 1.3 copy.12
Async XLA Ops:
  141.6 4.7 %copy-start.1 = (bf16[576,1792]{1,0:T(8,128)(2,1)S(1)}, bf16[576,1792]{1,0:T(8,128)(2,1)}, u32[]{:S(2)}) copy-start(bf16[576,1792]{1,0:T(8,128)(2,1)} %get-tuple-element.9) | copy-start | bytes 6193156
  146.3 2.3 %copy-start = (bf16[576,1792]{1,0:T(8,128)(2,1)S(1)}, bf16[576,1792]{1,0:T(8,128)(2,1)}, u32[]{:S(2)}) copy-start(bf16[576,1792]{1,0:T(8,128)(2,1)} %get-tuple-element.10) | copy-start | bytes 6193156

commit v2 on v0

v2 whole, which is shorter than its diff:
```python
import math

import jax
import jax.numpy as jnp
from jax import lax
from jax.experimental import pallas as pl
from jax.experimental.pallas import tpu as pltpu
from jax.sharding import PartitionSpec as P

MESH = pl.DeviceIdType.MESH
F32, BF16 = jnp.float32, jnp.bfloat16
ROWS, COLS, MATS, RDEV, CDEV = 576, 7168, 32, 18, 1792
ROUTER_ROWS = 384
LOADS = 6
MU_RATE, EPSILON = 0.95, 1e-07
COEF_A, COEF_B, COEF_C, ITERS = 3.4445, -4.775, 2.0315, 4
SCALE = 0.2 * math.sqrt(COLS)
VMEM_LIMIT = 58 * 1024 * 1024
EARLY = 24
MAIN = 512
OUT_PARTS = ((0, 256), (256, 768), (768, CDEV))
FIRST = [(r, t) for r in range(7) for t in range(r // 2 + 1)]
LAST = [(r, t) for r in (7, 8) for t in range(r // 2 + 1)]
Q_FIRST, Q_LAST = 8, 5


def dot(a, b):
    return jnp.dot(a, b, preferred_element_type=F32)


def dot_t(a, b):
    return lax.dot_general(a, b, (((1,), (1,)), ((), ())), preferred_element_type=F32)


def away(n):
    late = n // 16
    dy = (1 - late) * 2 * (n // 8) + late * (1 + 2 * ((n % 8) // 4))
    dz = (1 - late) * ((n // 2) % 4) + late * (2 * ((n // 2) % 2) + n // EARLY)
    return dy, dz, n % 2


def one_hot(match):
    return match.astype(F32).astype(BF16)


def halving_places(ex, c):
    near = ex + 1 - 2 * (ex % 2)
    far = 3 - ex
    first = (1 - c) * near + c * far
    second = (1 - c) * far + c * near

    def part(x):
        h = (1 - c) * (((x + 1) // 2) % 2) + c * (x // 2)
        q = (1 - c) * (x // 2) + c * (x % 2)
        return h, q
    return first, second, part


def kernel(owner_s, cls_s, g_hbm, m_hbm, nm_hbm, up_hbm, own_hbm,
           g, m, nm, zs, zmain, zlo, lor, x, ar1, ar2,
           perm_m, perm_l, back_m, back_l, order,
           part1, part2, got1a, got1b, got2a, got2b, full1, full2, gram, t_ref, coef,
           u, ulo, vmain, vlo, vl, up, own,
           in_sem, nm_sem, own_sem, up_sem, s1, r1, s2, r2, sm, rm, sl, rl, so, ro, slo, rlo, xs, xr):
    dp, ex = lax.axis_index("dp"), lax.axis_index("expert")
    y, z, c = dp // 8, (dp // 2) % 4, dp % 2

    def ahead(n):
        dy, dz, dc = away(n)
        return (((y + dy) % 4) * 4 + (z + dz) % 4) * 2 + (c + dc) % 2

    def behind(n):
        dy, dz, dc = away(n)
        return (((y + 4 - dy) % 4) * 4 + (z + 4 - dz) % 4) * 2 + (c + dc) % 2

    per = ROWS // LOADS
    loads = []
    for k in range(LOADS):
        rows = pl.ds(k * per, per)
        for n, (src, dst) in enumerate(((g_hbm, g), (m_hbm, m))):
            cp = pltpu.make_async_copy(src.at[rows], dst.at[rows], in_sem.at[n, k])
            cp.start()
            loads.append(cp)

    barrier = pltpu.get_barrier_semaphore()

    def greet(j, _):
        pl.semaphore_signal(barrier, inc=1, device_id=(ahead(j), ex), device_id_type=MESH)
        return _
    lax.fori_loop(1, 32, greet, 0)

    def greet_x(j, _):
        zz, xx = (z + j % 4) % 4, (ex + j // 4) % 4
        pl.semaphore_signal(barrier, inc=1, device_id=((y * 4 + zz) * 2 + c, xx), device_id_type=MESH)
        return _
    lax.fori_loop(4, 16, greet_x, 0)

    lane = lax.broadcasted_iota(jnp.int32, (8, ROWS), 1)
    mat = lax.broadcasted_iota(jnp.int32, (MATS, 128), 0)
    owner_row = jnp.zeros((8, ROWS), jnp.int32)
    cls = jnp.zeros((MATS, 128), F32)
    for i in range(MATS):
        owner_row = jnp.where(lane % MATS == i, owner_s[i], owner_row)
        cls = jnp.where(mat == i, cls_s[i].astype(F32), cls)
    wanted = (owner_row * RDEV + lane // MATS)[0:1]
    for k in range(16):
        o = lax.broadcasted_iota(jnp.int32, (32, MAIN), 0) + 32 * k
        perm_m[32 * k:32 * (k + 1), :] = one_hot((o // 16) * RDEV + o % 16 == wanted[:, :MAIN])
    o = lax.broadcasted_iota(jnp.int32, (64, 64), 0)
    perm_l[...] = one_hot((o // 2) * RDEV + 16 + o % 2 == wanted[:, MAIN:])

    def live_at(r):
        return jnp.where(dp * RDEV + r < ROUTER_ROWS, 1.0, 1.0 - cls)

    def rows_of(r):
        return pl.ds(pl.multiple_of(r * MATS, MATS), MATS)

    def stats(r, acc):
        live = live_at(r)
        gg, gm, mm = acc
        for t in range(CDEV // 128):
            cols = slice(t * 128, (t + 1) * 128)
            gv = g[rows_of(r), cols] * live
            mv = m[rows_of(r), cols] * (live * (MU_RATE * MU_RATE))
            gg, gm, mm = gg + gv * gv, gm + gv * mv, mm + mv * mv
        return gg, gm, mm

    acc = (jnp.zeros((MATS, 128), F32),) * 3
    for k in range(LOADS):
        loads[2 * k].wait()
        loads[2 * k + 1].wait()
        acc = lax.fori_loop(k * (RDEV // LOADS), (k + 1) * (RDEV // LOADS), stats, acc)
    sums = [jnp.sum(a, axis=1, keepdims=True) for a in acc]
    col = lax.broadcasted_iota(jnp.int32, (MATS, 128), 1)
    mine = jnp.where(col == 0, sums[0], jnp.where(col == 1, sums[1], jnp.where(col == 2, sums[2], 0.0)))
    mine = jnp.concatenate([mine, jnp.zeros((128 - MATS, 128), F32)], axis=0).T[:8]

    pl.semaphore_wait(barrier, 31 + 12)

    i1, i2 = y * 2 + c, ex * 4 + z
    ar1[i1] = mine

    def got(buf, slot, sem):
        return pltpu.make_async_copy(buf.at[slot], buf.at[slot], sem.at[slot])

    def one_of(j):
        return (y + j // 2) % 4, (c + j % 2) % 2

    def one(j):
        yy, cc = one_of(j)
        return pltpu.make_async_remote_copy(
            src_ref=ar1.at[i1], dst_ref=ar1.at[i1], send_sem=s1.at[j], recv_sem=r1.at[i1],
            device_id=((yy * 4 + z) * 2 + cc, ex), device_id_type=MESH)

    def two_of(j):
        return (z + j % 4) % 4, (ex + j // 4) % 4

    def two(j):
        zz, xx = two_of(j)
        return pltpu.make_async_remote_copy(
            src_ref=ar2.at[i2], dst_ref=ar2.at[i2], send_sem=s2.at[j], recv_sem=r2.at[i2],
            device_id=((y * 4 + zz) * 2 + c, xx), device_id_type=MESH)

    for j in range(1, 8):
        one(j).start()
    for j in range(1, 8):
        yy, cc = one_of(j)
        got(ar1, yy * 2 + cc, r1).wait()
    ar2[i2] = jnp.sum(ar1[...], axis=0)
    for j in range(1, 16):
        two(j).start()
    for j in range(1, 16):
        zz, xx = two_of(j)
        got(ar2, xx * 4 + zz, r2).wait()
    tot = jnp.concatenate([jnp.sum(ar2[...], axis=0), jnp.zeros((120, 128), F32)], axis=0).T[:MATS]
    gg, gm, mm = tot[:, 0:1], tot[:, 1:2], tot[:, 2:3]
    total = jnp.sum(gg, axis=0, keepdims=True)
    clip = jnp.minimum(1.0, jnp.sqrt(float(MATS * ROWS * COLS) / total))
    rate = (1.0 + MU_RATE) * clip
    sq = jnp.where(clip > 0.0, rate * rate * gg + 2.0 * rate * gm, 0.0) + mm
    norm = jnp.sqrt(jnp.maximum(sq, 0.0))
    inv = jnp.broadcast_to(1.0 / (norm + EPSILON), (MATS, 128))
    clip = jnp.broadcast_to(clip, (MATS, 128))

    def blend(r, _):
        live = live_at(r)
        lc = live * clip
        lm = live * MU_RATE
        for t in range(CDEV // 128):
            cols = slice(t * 128, (t + 1) * 128)
            gv = g[rows_of(r), cols] * lc
            nv = m[rows_of(r), cols] * lm + gv
            nm[rows_of(r), cols] = nv
            zs[rows_of(r), cols] = ((gv + MU_RATE * nv) * inv).astype(BF16)
        return _
    lax.fori_loop(0, RDEV, blend, 0)
    for t in range(CDEV // 256):
        cols = slice(t * 256, (t + 1) * 256)
        zmain[:, cols] = dot(perm_m[...], zs[:MAIN, cols]).astype(BF16)
        zlo[:, :, cols] = dot(perm_l[...], zs[MAIN:, cols]).reshape(MATS, 2, 256).astype(BF16)

    def block(ref, i):
        return ref.at[pl.ds(pl.multiple_of(i * 16, 16), 16)]

    def slot(ref, n):
        return block(ref, n + 4 * (n // EARLY))

    def main_in(n):
        to = ahead(n)
        return pltpu.make_async_remote_copy(
            src_ref=block(zmain, to), dst_ref=slot(x, n), send_sem=sm.at[n], recv_sem=rm.at[n],
            device_id=(to, ex), device_id_type=MESH)

    def lo_in(n):
        to = ahead(n)
        return pltpu.make_async_remote_copy(
            src_ref=zlo.at[to], dst_ref=lor.at[n], send_sem=sl.at[n], recv_sem=rl.at[n],
            device_id=(to, ex), device_id_type=MESH)

    def each(lo, hi, act):
        def step(n, _):
            act(n)
            return _
        lax.fori_loop(lo, hi, step, 0)

    each(1, 32, lambda n: lo_in(n).start())
    each(1, EARLY, lambda n: main_in(n).start())
    save_nm = pltpu.make_async_copy(nm, nm_hbm, nm_sem)
    save_nm.start()
    x[0:16, :] = zmain[pl.ds(pl.multiple_of(dp * 16, 16), 16), :]
    lor[0] = zlo[dp]

    owner_col = jnp.zeros((MATS, MAIN), jnp.int32)
    mats = lax.broadcasted_iota(jnp.int32, (MATS, MAIN), 0)
    for i in range(MATS):
        owner_col = jnp.where(mats == i, owner_s[i], owner_col)
    owner_col = owner_col * RDEV
    key = ((lane // 16) * RDEV + lane % 16)[0:1, :MAIN]
    for r in range(16):
        back_m[MATS * r:MATS * (r + 1), :] = one_hot(owner_col + r == key)
    key = ((lane // 2) * RDEV + 16 + lane % 2)[0:1, :64]
    for r in range(2):
        back_l[MATS * r:MATS * (r + 1), :] = one_hot(owner_col[:, :64] + (16 + r) == key)
    short = (lane >= 16 * EARLY) & (lane < 16 * EARLY + 64)
    n = jnp.where(short, (lane - 16 * EARLY) // 2, jnp.where(lane < 16 * EARLY, lane // 16, lane // 16 - 4))
    key = (behind(n) * RDEV + jnp.where(short, 16 + lane % 2, lane % 16))[0:1]
    for k in range(RDEV):
        rows = lax.broadcasted_iota(jnp.int32, (MATS, ROWS), 0) + MATS * k
        order[MATS * k:MATS * (k + 1), :] = one_hot(rows == key)

    each(1, EARLY, lambda n: main_in(n).wait_send())
    each(EARLY, 32, lambda n: main_in(n).start())

    def arrive(ref_at, sem, n):
        pltpu.make_async_copy(ref_at, ref_at, sem.at[n]).wait()

    each(1, EARLY, lambda n: arrive(slot(x, n), rm, n))
    each(1, 32, lambda n: arrive(lor.at[n], rl, n))
    x[16 * EARLY:16 * EARLY + 64, :] = lor[...].astype(F32).reshape(64, CDEV).astype(BF16)

    def put(part, n, piece):
        if piece.shape[1] < 128:
            piece = jnp.concatenate([piece, jnp.zeros((64, 128 - piece.shape[1]), F32)], axis=1)
        part[2 * n] = piece[:32]
        part[2 * n + 1] = piece[32:]

    top = 448
    for lo, hi in ((0, 256), (256, top)):
        gb = dot_t(x[lo:top, :], x[lo:hi, :])
        for n, (r, t) in enumerate(FIRST):
            if lo <= 128 * t < hi:
                put(part1, n, gb[64 * r - lo:64 * r - lo + 64, 128 * t - lo:min(128 * t + 128, hi) - lo])

    first, second, part_of = halving_places(ex, c)
    h, q = part_of(ex)
    h1, q1 = part_of(first)

    class Sum:
        def __init__(self, part, got_a, got_b, full, size, base):
            self.part, self.got_a, self.got_b, self.full, self.size, self.base = part, got_a, got_b, full, size, base

        def at(self, hh, qq):
            return pl.ds((2 * hh + qq) * self.size, self.size)

        def move(self, src, dst, n, to):
            return pltpu.make_async_remote_copy(
                src_ref=src, dst_ref=dst, send_sem=xs.at[self.base + n], recv_sem=xr.at[self.base + n],
                device_id=(dp, to), device_id_type=MESH)

        def halves(self):
            self.a1 = self.move(self.part.at[self.at(h1, 1 - q1)], self.got_a.at[0], 0, first)
            self.a2 = self.move(self.part.at[self.at(h1, q1)], self.got_a.at[1], 1, first)
            self.a1.start()
            self.a2.start()

        def quarters(self):
            self.a1.wait_recv()
            pass_on = self.at(h, 1 - q)
            self.part[pass_on] = self.part[pass_on] + self.got_a[0]
            self.b = self.move(self.part.at[pass_on], self.got_b, 2, second)
            self.b.start()

        def finish(self):
            self.a2.wait_recv()
            self.b.wait_recv()
            keep = self.at(h, q)
            self.full[keep] = self.part[keep] + self.got_a[1] + self.got_b[...]
            self.c1 = self.move(self.full.at[keep], self.full.at[keep], 3, second)
            self.c2 = self.move(self.full.at[keep], self.full.at[keep], 4, first)
            self.c1.start()
            self.c2.start()

        def forward(self):
            self.c1.wait_recv()
            other = self.at(h, 1 - q)
            self.c3 = self.move(self.full.at[other], self.full.at[other], 5, first)
            self.c3.start()

        def done(self):
            self.c2.wait_recv()
            self.c3.wait_recv()

        def sent(self):
            for cp in (self.a1, self.a2, self.b, self.c1, self.c2, self.c3):
                cp.wait_send()

    def lay_out(panels, full):
        for n, (r, t) in enumerate(panels):
            w = min(128, ROWS - 128 * t)
            piece = jnp.concatenate([full[2 * n], full[2 * n + 1]], axis=0)
            if 128 * t + 128 > top and r < 7:
                w = top - 128 * t
            gram[64 * r:64 * r + 64, 128 * t:128 * t + w] = piece[:, :w]
            if 128 * t + w <= 64 * r:
                gram[128 * t:128 * t + w, 64 * r:64 * r + 64] = piece.T[:w]
            elif 128 * t < 64 * r:
                gram[128 * t:64 * r, 64 * r:64 * r + 64] = piece.T[:64 * r - 128 * t]

    e1 = Sum(part1, got1a, got1b, full1, Q_FIRST, 0)
    e2 = Sum(part2, got2a, got2b, full2, Q_LAST, 6)
    e1.halves()
    e1.quarters()
    each(EARLY, 32, lambda n: arrive(slot(x, n), rm, n))
    gb = dot_t(x[top:, :], x[...])
    for n, (r, t) in enumerate(LAST):
        put(part2, n, gb[64 * r - top:64 * r - top + 64, 128 * t:min(128 * t + 128, ROWS)])
    for n in range(2 * len(LAST), 4 * Q_LAST):
        part2[n] = jnp.zeros((32, 128), F32)
    e2.halves()
    e1.finish()
    e2.quarters()
    e1.forward()
    e2.finish()
    e1.done()
    lay_out(FIRST, full1)
    e2.forward()
    e2.done()
    lay_out(LAST, full2)

    for k in range(ITERS):
        a16 = gram[...].astype(BF16)
        b16 = (COEF_B * a16.astype(F32) + COEF_C * dot(a16, a16)).astype(BF16)
        coef[k] = b16
        if k + 1 < ITERS:
            low = (gram[...] - a16.astype(F32)).astype(BF16)
            t_ref[...] = COEF_A * gram[...] + (dot(a16, b16) + dot(low, b16))
            t16 = t_ref[...].astype(BF16)
            tlow = (t_ref[...] - t16.astype(F32)).astype(BF16)
            gram[...] = COEF_A * t_ref[...] + (dot(b16, t16) + dot(b16, tlow))

    def main_out(p, n):
        to = behind(n)
        cols = pl.ds(OUT_PARTS[p][0], OUT_PARTS[p][1] - OUT_PARTS[p][0])
        return pltpu.make_async_remote_copy(
            src_ref=u.at[pl.ds(pl.multiple_of((n + 4 * (n // EARLY)) * 16, 16), 16), cols],
            dst_ref=vmain.at[pl.ds(pl.multiple_of(dp * 16, 16), 16), cols],
            send_sem=so.at[p, n], recv_sem=ro.at[p, n], device_id=(to, ex), device_id_type=MESH)

    def lo_out(n):
        to = behind(n)
        return pltpu.make_async_remote_copy(
            src_ref=ulo.at[n], dst_ref=vlo.at[dp], send_sem=slo.at[n], recv_sem=rlo.at[n],
            device_id=(to, ex), device_id_type=MESH)

    for p, (lo, hi) in enumerate(OUT_PARTS):
        for at in range(lo, hi, 512):
            cols = slice(at, min(at + 512, hi))
            cur = x[:, cols]
            for k in range(ITERS):
                out = COEF_A * cur.astype(F32) + dot(coef[k], cur)
                if k + 1 < ITERS:
                    cur = out.astype(BF16)
            res = (SCALE * out).astype(BF16)
            u[:, cols] = res
            ulo[:, :, cols] = res[16 * EARLY:16 * EARLY + 64].astype(F32).reshape(MATS, 2, cols.stop - at).astype(BF16)
        each(1, 32, lambda n, p=p: main_out(p, n).start())
    each(1, 32, lambda n: lo_out(n).start())

    vmain[pl.ds(pl.multiple_of(dp * 16, 16), 16), :] = u[0:16, :]
    vlo[dp] = ulo[0]
    for t in range(CDEV // 256):
        cols = slice(t * 256, (t + 1) * 256)
        own[:, cols] = dot(order[...], u[:, cols]).astype(BF16)
    save_own = pltpu.make_async_copy(own, own_hbm, own_sem)
    save_own.start()

    saves = []
    for p, (lo, hi) in enumerate(OUT_PARTS):
        part_cols = pl.ds(lo, hi - lo)

        def landed(n, p=p, part_cols=part_cols):
            at = vmain.at[pl.ds(pl.multiple_of(ahead(n) * 16, 16), 16), part_cols]
            pltpu.make_async_copy(at, at, ro.at[p, n]).wait()
        each(1, 32, landed)
        for at in range(lo, hi, 256):
            cols = slice(at, at + 256)
            up[:MAIN, cols] = dot(back_m[...], vmain[:, cols]).astype(BF16)
        cp = pltpu.make_async_copy(up.at[pl.ds(0, MAIN), part_cols], up_hbm.at[pl.ds(0, MAIN), part_cols], up_sem.at[p])
        cp.start()
        saves.append(cp)
    each(1, 32, lambda n: arrive(vlo.at[ahead(n)], rlo, n))
    vl[...] = vlo[...].astype(F32).reshape(64, CDEV).astype(BF16)
    up[MAIN:, :] = dot(back_l[...], vl[...]).astype(BF16)
    cp = pltpu.make_async_copy(up.at[pl.ds(MAIN, 64)], up_hbm.at[pl.ds(MAIN, 64)], up_sem.at[len(OUT_PARTS)])
    cp.start()
    saves.append(cp)

    for j in range(1, 8):
        one(j).wait_send()
    for j in range(1, 16):
        two(j).wait_send()
    each(1, 32, lambda n: lo_in(n).wait_send())
    each(EARLY, 32, lambda n: main_in(n).wait_send())
    e1.sent()
    e2.sent()
    for p in range(len(OUT_PARTS)):
        each(1, 32, lambda n, p=p: main_out(p, n).wait_send())
    each(1, 32, lambda n: lo_out(n).wait_send())
    save_nm.wait()
    save_own.wait()
    for cp in saves:
        cp.wait()


def step(owner, cls, g, m):
    D, V = pltpu.SemaphoreType.DMA, pltpu.VMEM
    wide = (ROWS, CDEV)
    square = (ROWS, ROWS)
    return pl.pallas_call(
        kernel,
        out_shape=(jax.ShapeDtypeStruct(wide, F32), jax.ShapeDtypeStruct(wide, BF16), jax.ShapeDtypeStruct(wide, BF16)),
        in_specs=[pl.BlockSpec(memory_space=pltpu.SMEM)] * 2 + [pl.BlockSpec(memory_space=pl.ANY)] * 2,
        out_specs=(pl.BlockSpec(memory_space=pl.ANY),) * 3,
        scratch_shapes=[
            V(wide, F32), V(wide, F32), V(wide, F32), V(wide, BF16),
            V((MAIN, CDEV), BF16), V((MATS, 2, CDEV), BF16), V((MATS, 2, CDEV), BF16), V(wide, BF16),
            V((8, 8, 128), F32), V((16, 8, 128), F32),
            V((MAIN, MAIN), BF16), V((64, 64), BF16), V((MAIN, MAIN), BF16), V((64, 64), BF16), V(square, BF16),
            V((4 * Q_FIRST, 32, 128), F32), V((4 * Q_LAST, 32, 128), F32),
            V((2, Q_FIRST, 32, 128), F32), V((Q_FIRST, 32, 128), F32),
            V((2, Q_LAST, 32, 128), F32), V((Q_LAST, 32, 128), F32),
            V((4 * Q_FIRST, 32, 128), F32), V((4 * Q_LAST, 32, 128), F32),
            V(square, F32), V(square, F32), V((ITERS, ROWS, ROWS), BF16),
            V(wide, BF16), V((MATS, 2, CDEV), BF16), V((MAIN, CDEV), BF16), V((MATS, 2, CDEV), BF16), V((64, CDEV), BF16),
            V(wide, BF16), V(wide, BF16),
            D((2, LOADS)), D, D, D((len(OUT_PARTS) + 1,)),
            D((8,)), D((8,)), D((16,)), D((16,)), D((32,)), D((32,)), D((32,)), D((32,)),
            D((len(OUT_PARTS), 32)), D((len(OUT_PARTS), 32)), D((32,)), D((32,)), D((12,)), D((12,)),
        ],
        compiler_params=pltpu.CompilerParams(collective_id=0, has_side_effects=True, vmem_limit_bytes=VMEM_LIMIT),
    )(owner, cls, g, m)


PIECES = 4


def place_kernel(*refs):
    sems = refs[6]
    copies = []
    for i in range(3):
        for k in range(PIECES):
            rows = pl.ds(k * (ROWS // PIECES), ROWS // PIECES)
            copies.append(pltpu.make_async_copy(refs[i].at[rows], refs[3 + i].at[rows], sems.at[i, k]))
    for cp in copies:
        cp.start()
    for cp in copies:
        cp.wait()


def placed(*arrays):
    return pl.pallas_call(
        place_kernel,
        out_shape=tuple(jax.ShapeDtypeStruct(a.shape, a.dtype) for a in arrays),
        in_specs=[pl.BlockSpec(memory_space=pl.ANY)] * 3,
        out_specs=(pl.BlockSpec(memory_space=pl.ANY),) * 3,
        scratch_shapes=[pltpu.SemaphoreType.DMA((3, PIECES))],
    )(*arrays)


def body(gradient, momentum, owner_table, shape_class):
    g = jnp.transpose(gradient, (1, 0, 2)).reshape(ROWS, CDEV)
    m = jnp.transpose(momentum, (1, 0, 2)).reshape(ROWS, CDEV)
    nm, up, own = placed(*step(owner_table, shape_class, g, m))
    new_moment = jnp.transpose(nm.reshape(RDEV, MATS, CDEV), (1, 0, 2))
    update = jnp.transpose(up.reshape(RDEV, MATS, CDEV), (1, 0, 2))
    return new_moment, update, own[None]


def solution(mesh):
    return jax.shard_map(
        body,
        mesh=mesh,
        in_specs=(P(None, "dp", "expert"), P(None, "dp", "expert"), P(), P()),
        out_specs=(P(None, "dp", "expert"), P(None, "dp", "expert"), P("dp", None, "expert")),
        check_vma=False,
    )
```

time: 443 us -> 368 us (0.83)
  Pallas kernels: 0 us -> 367 us
  blocking collectives: 286 us -> 0 us
  matrix products: 42.9 us -> 0 us
  local copies, waits for them, and re-layouts: 36.7 us -> 0 us
  waiting for transfers between devices: 27.9 us -> 0 us
  other arithmetic: 25.1 us -> 0 us
  starting transfers between devices: 22 us -> 0 us
    pallas_call x0 -> x2, Pallas kernels: none -> 367 us  [the longest x1 251 us: placed(): pl.pallas_call(place_kernel, out_shape=tuple((jax.ShapeDtypeStruct(a.shap...]
    psum x6 -> x0, blocking collectives: 245 us -> none  [the longest x4 114 us: gram_of(): full = lax.psum(local, 'expert')]
    dot_general x9 -> x0, matrix products: 42.9 us -> none  [the longest x4 22.5 us: orthogonalize(): jnp.dot(poly, current, preferred_element_type=jnp.float32)]
    all_to_all x1 -> x0, blocking collectives: 40.6 us -> none  [body(): lax.all_to_all(outgoing, 'dp', split_axis=0, concat_axis=2, tiled=True)]
    all_to_all x1 -> x0, waiting for transfers between devices: 27.9 us -> none  [body(): lax.all_to_all(mapped, 'dp', split_axis=2, concat_axis=0, tiled=True)]
    all_to_all x1 -> x0, starting transfers between devices: 22 us -> none  [body(): lax.all_to_all(mapped, 'dp', split_axis=2, concat_axis=0, tiled=True)]
    unnamed x1 -> x0, other arithmetic: 13.2 us -> none
    all_to_all x1 -> x0, local copies, waits for them, and re-layouts: 13.1 us -> none  [body(): lax.all_to_all(mapped, 'dp', split_axis=2, concat_axis=0, tiled=True)]
  transfers between devices with their start and end apart: 1 -> 0, of which waited for: 1 -> 0; matrix products, arithmetic and copies ran while one was open for 0% -> 0% of each run, Pallas kernels for 0% -> 0%
where the time goes in v2:
time: 368 us; the launch traced here: 367 us
  Pallas kernels  367 us (100%)
    pallas_call x1, Pallas kernels, placed(): pl.pallas_call(place_kernel, out_shape=tuple((jax.ShapeDtypeStruct(a.shap...  251 us
    pallas_call x1, Pallas kernels, step(): pl.pallas_call(kernel, out_shape=(jax.ShapeDtypeStruct(wide, F32), jax.Sh...  115 us

profile of v2, /device:TPU:1, one launch (start us, length us, event | category | flops | bytes accessed | tf_op | source)
XLA Modules:
  0.0 367.4 jit_solution(3927200160380046132)
XLA Ops:
  0.6 115.3 %shard_map.67 = (f32[576,1792]{1,0:T(8,128)}, bf16[576,1792]{1,0:T(8,128)(2,1)}, bf16[576,1792]{1,0:T(8,128)(2,1)}) custom-call(s32[32]{0:T(128)} %owner_s.1, s32[32]{0:T(128)} %cls_s.1, f32[576,1792]{1,0:T(8,128)} %bitcast.13, f32[576,1792]{1,0:T(8,128)} %bitcast.14), custom_call_target="tpu_custom_call" | custom-call | tf_op jit(solution)/shard_map/pallas_call | solution.py:449
  115.9 251.4 %shard_map.68 = (f32[576,1792]{1,0:T(8,128)}, bf16[576,1792]{1,0:T(8,128)(2,1)}, bf16[576,1792]{1,0:T(8,128)(2,1)}) custom-call(f32[576,1792]{1,0:T(8,128)} %get-tuple-element.9.refs_0_, bf16[576,1792]{1,0:T(8,128)(2,1)} %get-tuple-element.10.refs_1_, bf16[576,1792]{1,0:T(8,128)(2,1)} %get-tuple-element.11.refs_2_), custom_call_target="tpu_custom_call" | custom-call | tf_op jit(solution)/shard_map/pallas_call | solution.py:491

commit v3 on v2

--- a/solution.py
+++ b/solution.py
@@ -15,13 +15,20 @@
 MU_RATE, EPSILON = 0.95, 1e-07
 COEF_A, COEF_B, COEF_C, ITERS = 3.4445, -4.775, 2.0315, 4
 SCALE = 0.2 * math.sqrt(COLS)
-VMEM_LIMIT = 58 * 1024 * 1024
-EARLY = 24
+VMEM_LIMIT = 44 * 1024 * 1024
 MAIN = 512
 OUT_PARTS = ((0, 256), (256, 768), (768, CDEV))
-FIRST = [(r, t) for r in range(7) for t in range(r // 2 + 1)]
-LAST = [(r, t) for r in (7, 8) for t in range(r // 2 + 1)]
-Q_FIRST, Q_LAST = 8, 5
+WINDOW = 12
+PAIRS = ((0, 0), (2, 2), (1, 0), (0, 1), (3, 0), (0, 3), (2, 0), (0, 2),
+         (1, 2), (2, 1), (3, 2), (2, 3),
+         (1, 1), (3, 3), (1, 3), (3, 1))
+SLOTS = tuple((dy, dz, dc) for dy, dz in PAIRS for dc in (0, 1))
+GROUPS = (16, 24, 32)
+SHORT = 16 * GROUPS[0]
+TOPS = (SHORT + 64, 16 * GROUPS[1] + 64, ROWS)
+PANELS = tuple(tuple((r, t) for r in range(lo // 64, hi // 64) for t in range(r // 2 + 1))
+               for lo, hi in zip((0,) + TOPS, TOPS))
+QUARTERS = tuple(-(-2 * len(p) // 4) for p in PANELS)
 
 
 def dot(a, b):
@@ -30,13 +37,6 @@
 
 def dot_t(a, b):
     return lax.dot_general(a, b, (((1,), (1,)), ((), ())), preferred_element_type=F32)
-
-
-def away(n):
-    late = n // 16
-    dy = (1 - late) * 2 * (n // 8) + late * (1 + 2 * ((n % 8) // 4))
-    dz = (1 - late) * ((n // 2) % 4) + late * (2 * ((n // 2) % 2) + n // EARLY)
-    return dy, dz, n % 2
 
 
 def one_hot(match):
@@ -56,21 +56,25 @@
     return first, second, part
 
 
+def row_at(n):
+    return 16 * n + (64 if n >= GROUPS[0] else 0)
+
+
 def kernel(owner_s, cls_s, g_hbm, m_hbm, nm_hbm, up_hbm, own_hbm,
            g, m, nm, zs, zmain, zlo, lor, x, ar1, ar2,
-           perm_m, perm_l, back_m, back_l, order,
-           part1, part2, got1a, got1b, got2a, got2b, full1, full2, gram, t_ref, coef,
-           u, ulo, vmain, vlo, vl, up, own,
-           in_sem, nm_sem, own_sem, up_sem, s1, r1, s2, r2, sm, rm, sl, rl, so, ro, slo, rlo, xs, xr):
+           perm_m, perm_l, back_m, back_l, order, *rest):
+    sums = [rest[4 * i:4 * i + 4] for i in range(3)]
+    (gram, t_ref, left, right, coef, u, ulo, vmain, vlo, vl, up, own,
+     in_sem, nm_sem, own_sem, up_sem, s1, r1, s2, r2, sm, rm, sl, rl, so, ro, slo, rlo, xs, xr) = rest[12:]
     dp, ex = lax.axis_index("dp"), lax.axis_index("expert")
     y, z, c = dp // 8, (dp // 2) % 4, dp % 2
 
     def ahead(n):
-        dy, dz, dc = away(n)
+        dy, dz, dc = SLOTS[n]
         return (((y + dy) % 4) * 4 + (z + dz) % 4) * 2 + (c + dc) % 2
 
     def behind(n):
-        dy, dz, dc = away(n)
+        dy, dz, dc = SLOTS[n]
         return (((y + 4 - dy) % 4) * 4 + (z + 4 - dz) % 4) * 2 + (c + dc) % 2
 
     per = ROWS // LOADS
@@ -85,7 +89,8 @@
     barrier = pltpu.get_barrier_semaphore()
 
     def greet(j, _):
-        pl.semaphore_signal(barrier, inc=1, device_id=(ahead(j), ex), device_id_type=MESH)
+        to = (((y + j // 8) % 4) * 4 + (z + (j // 2) % 4) % 4) * 2 + (c + j % 2) % 2
+        pl.semaphore_signal(barrier, inc=1, device_id=(to, ex), device_id_type=MESH)
         return _
     lax.fori_loop(1, 32, greet, 0)
 
@@ -103,9 +108,10 @@
         owner_row = jnp.where(lane % MATS == i, owner_s[i], owner_row)
         cls = jnp.where(mat == i, cls_s[i].astype(F32), cls)
     wanted = (owner_row * RDEV + lane // MATS)[0:1]
+    o = lax.broadcasted_iota(jnp.int32, (32, MAIN), 0)
+    key = (o // 16) * RDEV + o % 16
     for k in range(16):
-        o = lax.broadcasted_iota(jnp.int32, (32, MAIN), 0) + 32 * k
-        perm_m[32 * k:32 * (k + 1), :] = one_hot((o // 16) * RDEV + o % 16 == wanted[:, :MAIN])
+        perm_m[32 * k:32 * (k + 1), :] = one_hot(key + 2 * RDEV * k == wanted[:, :MAIN])
     o = lax.broadcasted_iota(jnp.int32, (64, 64), 0)
     perm_l[...] = one_hot((o // 2) * RDEV + 16 + o % 2 == wanted[:, MAIN:])
 
@@ -130,9 +136,9 @@
         loads[2 * k].wait()
         loads[2 * k + 1].wait()
         acc = lax.fori_loop(k * (RDEV // LOADS), (k + 1) * (RDEV // LOADS), stats, acc)
-    sums = [jnp.sum(a, axis=1, keepdims=True) for a in acc]
+    tots = [jnp.sum(a, axis=1, keepdims=True) for a in acc]
     col = lax.broadcasted_iota(jnp.int32, (MATS, 128), 1)
-    mine = jnp.where(col == 0, sums[0], jnp.where(col == 1, sums[1], jnp.where(col == 2, sums[2], 0.0)))
+    mine = jnp.where(col == 0, tots[0], jnp.where(col == 1, tots[1], jnp.where(col == 2, tots[2], 0.0)))
     mine = jnp.concatenate([mine, jnp.zeros((128 - MATS, 128), F32)], axis=0).T[:8]
 
     pl.semaphore_wait(barrier, 31 + 12)
@@ -203,7 +209,7 @@
         return ref.at[pl.ds(pl.multiple_of(i * 16, 16), 16)]
 
     def slot(ref, n):
-        return block(ref, n + 4 * (n // EARLY))
+        return ref.at[pl.ds(row_at(n), 16)]
 
     def main_in(n):
         to = ahead(n)
@@ -218,13 +224,16 @@
             device_id=(to, ex), device_id_type=MESH)
 
     def each(lo, hi, act):
-        def step(n, _):
+        for n in range(lo, hi):
             act(n)
-            return _
-        lax.fori_loop(lo, hi, step, 0)
+
+    def go(n):
+        if n > WINDOW:
+            main_in(n - WINDOW).wait_send()
+        main_in(n).start()
 
     each(1, 32, lambda n: lo_in(n).start())
-    each(1, EARLY, lambda n: main_in(n).start())
+    each(1, WINDOW + 1, go)
     save_nm = pltpu.make_async_copy(nm, nm_hbm, nm_sem)
     save_nm.start()
     x[0:16, :] = zmain[pl.ds(pl.multiple_of(dp * 16, 16), 16), :]
@@ -241,22 +250,24 @@
     key = ((lane // 2) * RDEV + 16 + lane % 2)[0:1, :64]
     for r in range(2):
         back_l[MATS * r:MATS * (r + 1), :] = one_hot(owner_col[:, :64] + (16 + r) == key)
-    short = (lane >= 16 * EARLY) & (lane < 16 * EARLY + 64)
-    n = jnp.where(short, (lane - 16 * EARLY) // 2, jnp.where(lane < 16 * EARLY, lane // 16, lane // 16 - 4))
-    key = (behind(n) * RDEV + jnp.where(short, 16 + lane % 2, lane % 16))[0:1]
+    short = (lane >= SHORT) & (lane < SHORT + 64)
+    n = jnp.where(short, (lane - SHORT) // 2, jnp.where(lane < SHORT, lane // 16, lane // 16 - 4))
+    source = jnp.zeros((8, ROWS), jnp.int32)
+    for k in range(32):
+        source = jnp.where(n == k, behind(k), source)
+    key = (source * RDEV + jnp.where(short, 16 + lane % 2, lane % 16))[0:1]
     for k in range(RDEV):
         rows = lax.broadcasted_iota(jnp.int32, (MATS, ROWS), 0) + MATS * k
         order[MATS * k:MATS * (k + 1), :] = one_hot(rows == key)
 
-    each(1, EARLY, lambda n: main_in(n).wait_send())
-    each(EARLY, 32, lambda n: main_in(n).start())
+    each(WINDOW + 1, GROUPS[0] + WINDOW, go)
 
     def arrive(ref_at, sem, n):
         pltpu.make_async_copy(ref_at, ref_at, sem.at[n]).wait()
 
-    each(1, EARLY, lambda n: arrive(slot(x, n), rm, n))
+    each(1, GROUPS[0], lambda n: arrive(slot(x, n), rm, n))
     each(1, 32, lambda n: arrive(lor.at[n], rl, n))
-    x[16 * EARLY:16 * EARLY + 64, :] = lor[...].astype(F32).reshape(64, CDEV).astype(BF16)
+    x[SHORT:SHORT + 64, :] = lor[...].astype(F32).reshape(64, CDEV).astype(BF16)
 
     def put(part, n, piece):
         if piece.shape[1] < 128:
@@ -264,12 +275,17 @@
         part[2 * n] = piece[:32]
         part[2 * n + 1] = piece[32:]
 
-    top = 448
-    for lo, hi in ((0, 256), (256, top)):
-        gb = dot_t(x[lo:top, :], x[lo:hi, :])
-        for n, (r, t) in enumerate(FIRST):
-            if lo <= 128 * t < hi:
-                put(part1, n, gb[64 * r - lo:64 * r - lo + 64, 128 * t - lo:min(128 * t + 128, hi) - lo])
+    def terms(i, part):
+        low, top = (0,) + TOPS[:2], TOPS[i]
+        low = low[i]
+        for lo, hi in (((0, 256), (256, top)) if i == 0 else ((0, top),)):
+            lo_row = max(low, lo)
+            gb = dot_t(x[lo_row:top, :], x[lo:hi, :])
+            for n, (r, t) in enumerate(PANELS[i]):
+                if lo <= 128 * t < hi:
+                    put(part, n, gb[64 * r - lo_row:64 * r - lo_row + 64, 128 * t - lo:min(128 * t + 128, hi) - lo])
+        for n in range(2 * len(PANELS[i]), 4 * QUARTERS[i]):
+            part[n] = jnp.zeros((32, 128), F32)
 
     first, second, part_of = halving_places(ex, c)
     h, q = part_of(ex)
@@ -324,55 +340,68 @@
             for cp in (self.a1, self.a2, self.b, self.c1, self.c2, self.c3):
                 cp.wait_send()
 
-    def lay_out(panels, full):
-        for n, (r, t) in enumerate(panels):
-            w = min(128, ROWS - 128 * t)
+    def lay_out(i, full):
+        for n, (r, t) in enumerate(PANELS[i]):
+            w = min(128, TOPS[i] - 128 * t)
             piece = jnp.concatenate([full[2 * n], full[2 * n + 1]], axis=0)
-            if 128 * t + 128 > top and r < 7:
-                w = top - 128 * t
             gram[64 * r:64 * r + 64, 128 * t:128 * t + w] = piece[:, :w]
             if 128 * t + w <= 64 * r:
                 gram[128 * t:128 * t + w, 64 * r:64 * r + 64] = piece.T[:w]
             elif 128 * t < 64 * r:
                 gram[128 * t:64 * r, 64 * r:64 * r + 64] = piece.T[:64 * r - 128 * t]
 
-    e1 = Sum(part1, got1a, got1b, full1, Q_FIRST, 0)
-    e2 = Sum(part2, got2a, got2b, full2, Q_LAST, 6)
+    e1, e2, e3 = (Sum(*sums[i], QUARTERS[i], 6 * i) for i in range(3))
+    terms(0, e1.part)
     e1.halves()
+    each(GROUPS[0] + WINDOW, 32, go)
     e1.quarters()
-    each(EARLY, 32, lambda n: arrive(slot(x, n), rm, n))
-    gb = dot_t(x[top:, :], x[...])
-    for n, (r, t) in enumerate(LAST):
-        put(part2, n, gb[64 * r - top:64 * r - top + 64, 128 * t:min(128 * t + 128, ROWS)])
-    for n in range(2 * len(LAST), 4 * Q_LAST):
-        part2[n] = jnp.zeros((32, 128), F32)
+    each(GROUPS[0], GROUPS[1], lambda n: arrive(slot(x, n), rm, n))
+    terms(1, e2.part)
     e2.halves()
     e1.finish()
     e2.quarters()
     e1.forward()
+    each(GROUPS[1], 32, lambda n: arrive(slot(x, n), rm, n))
+    terms(2, e3.part)
+    e3.halves()
     e2.finish()
     e1.done()
-    lay_out(FIRST, full1)
+    lay_out(0, e1.full)
     e2.forward()
+    e3.quarters()
     e2.done()
-    lay_out(LAST, full2)
-
+    lay_out(1, e2.full)
+    e3.finish()
+    e3.forward()
+    e3.done()
+    lay_out(2, e3.full)
+
+    left[:, ROWS:640] = jnp.zeros((ROWS, 64), BF16)
+    left[:, 640 + ROWS:] = jnp.zeros((ROWS, 64), BF16)
+    right[ROWS:640, :] = jnp.zeros((64, ROWS), BF16)
+    right[640 + ROWS:, :] = jnp.zeros((64, ROWS), BF16)
     for k in range(ITERS):
         a16 = gram[...].astype(BF16)
         b16 = (COEF_B * a16.astype(F32) + COEF_C * dot(a16, a16)).astype(BF16)
         coef[k] = b16
         if k + 1 < ITERS:
-            low = (gram[...] - a16.astype(F32)).astype(BF16)
-            t_ref[...] = COEF_A * gram[...] + (dot(a16, b16) + dot(low, b16))
+            left[:, :ROWS] = a16
+            left[:, 640:640 + ROWS] = (gram[...] - a16.astype(F32)).astype(BF16)
+            right[:ROWS, :] = b16
+            right[640:640 + ROWS, :] = b16
+            t_ref[...] = COEF_A * gram[...] + dot(left[...], right[...])
+            left[:, :ROWS] = b16
+            left[:, 640:640 + ROWS] = b16
             t16 = t_ref[...].astype(BF16)
-            tlow = (t_ref[...] - t16.astype(F32)).astype(BF16)
-            gram[...] = COEF_A * t_ref[...] + (dot(b16, t16) + dot(b16, tlow))
+            right[:ROWS, :] = t16
+            right[640:640 + ROWS, :] = (t_ref[...] - t16.astype(F32)).astype(BF16)
+            gram[...] = COEF_A * t_ref[...] + dot(left[...], right[...])
 
     def main_out(p, n):
         to = behind(n)
         cols = pl.ds(OUT_PARTS[p][0], OUT_PARTS[p][1] - OUT_PARTS[p][0])
         return pltpu.make_async_remote_copy(
-            src_ref=u.at[pl.ds(pl.multiple_of((n + 4 * (n // EARLY)) * 16, 16), 16), cols],
+            src_ref=u.at[pl.ds(row_at(n), 16), cols],
             dst_ref=vmain.at[pl.ds(pl.multiple_of(dp * 16, 16), 16), cols],
             send_sem=so.at[p, n], recv_sem=ro.at[p, n], device_id=(to, ex), device_id_type=MESH)
 
@@ -392,7 +421,7 @@
                     cur = out.astype(BF16)
             res = (SCALE * out).astype(BF16)
             u[:, cols] = res
-            ulo[:, :, cols] = res[16 * EARLY:16 * EARLY + 64].astype(F32).reshape(MATS, 2, cols.stop - at).astype(BF16)
+            ulo[:, :, cols] = res[SHORT:SHORT + 64].astype(F32).reshape(MATS, 2, cols.stop - at).astype(BF16)
         each(1, 32, lambda n, p=p: main_out(p, n).start())
     each(1, 32, lambda n: lo_out(n).start())
 
@@ -430,9 +459,9 @@
     for j in range(1, 16):
         two(j).wait_send()
     each(1, 32, lambda n: lo_in(n).wait_send())
-    each(EARLY, 32, lambda n: main_in(n).wait_send())
-    e1.sent()
-    e2.sent()
+    each(32 - WINDOW, 32, lambda n: main_in(n).wait_send())
+    for e in (e1, e2, e3):
+        e.sent()
     for p in range(len(OUT_PARTS)):
         each(1, 32, lambda n, p=p: main_out(p, n).wait_send())
     each(1, 32, lambda n: lo_out(n).wait_send())
@@ -456,16 +485,13 @@
             V((MAIN, CDEV), BF16), V((MATS, 2, CDEV), BF16), V((MATS, 2, CDEV), BF16), V(wide, BF16),
             V((8, 8, 128), F32), V((16, 8, 128), F32),
             V((MAIN, MAIN), BF16), V((64, 64), BF16), V((MAIN, MAIN), BF16), V((64, 64), BF16), V(square, BF16),
-            V((4 * Q_FIRST, 32, 128), F32), V((4 * Q_LAST, 32, 128), F32),
-            V((2, Q_FIRST, 32, 128), F32), V((Q_FIRST, 32, 128), F32),
-            V((2, Q_LAST, 32, 128), F32), V((Q_LAST, 32, 128), F32),
-            V((4 * Q_FIRST, 32, 128), F32), V((4 * Q_LAST, 32, 128), F32),
-            V(square, F32), V(square, F32), V((ITERS, ROWS, ROWS), BF16),
+            *[V((k * q, 32, 128), F32) if k else V((2, q, 32, 128), F32) for q in QUARTERS for k in (4, 0, 1, 4)],
+            V(square, F32), V(square, F32), V((ROWS, 1280), BF16), V((1280, ROWS), BF16), V((ITERS, ROWS, ROWS), BF16),
             V(wide, BF16), V((MATS, 2, CDEV), BF16), V((MAIN, CDEV), BF16), V((MATS, 2, CDEV), BF16), V((64, CDEV), BF16),
             V(wide, BF16), V(wide, BF16),
             D((2, LOADS)), D, D, D((len(OUT_PARTS) + 1,)),
             D((8,)), D((8,)), D((16,)), D((16,)), D((32,)), D((32,)), D((32,)), D((32,)),
-            D((len(OUT_PARTS), 32)), D((len(OUT_PARTS), 32)), D((32,)), D((32,)), D((12,)), D((12,)),
+            D((len(OUT_PARTS), 32)), D((len(OUT_PARTS), 32)), D((32,)), D((32,)), D((18,)), D((18,)),
         ],
         compiler_params=pltpu.CompilerParams(collective_id=0, has_side_effects=True, vmem_limit_bytes=VMEM_LIMIT),
     )(owner, cls, g, m)
@@ -475,12 +501,11 @@
 
 
 def place_kernel(*refs):
-    sems = refs[6]
     copies = []
     for i in range(3):
         for k in range(PIECES):
             rows = pl.ds(k * (ROWS // PIECES), ROWS // PIECES)
-            copies.append(pltpu.make_async_copy(refs[i].at[rows], refs[3 + i].at[rows], sems.at[i, k]))
+            copies.append(pltpu.make_async_copy(refs[i].at[rows], refs[3 + i].at[rows], refs[6].at[i, k]))
     for cp in copies:
         cp.start()
     for cp in copies:

time: 368 us -> 369 us (level)
  Pallas kernels: 367 us -> 361 us
  local copies, waits for them, and re-layouts: 0 us -> 5.86 us
    unnamed x0 -> x10, local copies, waits for them, and re-layouts: none -> 5.86 us
    pallas_call x1, Pallas kernels: 115 us -> 110 us  [step(): pl.pallas_call(kernel, out_shape=(jax.ShapeDtypeStruct(wide, F32), jax.Sh...]
where the time goes in v3:
time: 369 us; the launch traced here: 368 us
  Pallas kernels  361 us (98%)
  local copies, waits for them, and re-layouts  5.86 us (2%)
    pallas_call x1, Pallas kernels, placed(): pl.pallas_call(place_kernel, out_shape=tuple((jax.ShapeDtypeStruct(a.shap...  251 us
    pallas_call x1, Pallas kernels, step(): pl.pallas_call(kernel, out_shape=(jax.ShapeDtypeStruct(wide, F32), jax.Sh...  110 us

profile of v3, /device:TPU:1, one launch (start us, length us, event | category | flops | bytes accessed | tf_op | source)
XLA Modules:
  0.0 368.2 jit_solution(9005312326289778288)
XLA Ops:
  0.6 0.0 copy-start.3
  0.6 0.6 copy-done.3
  1.3 0.0 copy-start.4
  1.3 0.7 copy-done.4
  1.9 110.1 %shard_map.67 = (f32[576,1792]{1,0:T(8,128)S(1)}, bf16[576,1792]{1,0:T(8,128)(2,1)S(1)}, bf16[576,1792]{1,0:T(8,128)(2,1)S(1)}) custom-call(s32[32]{0:T(128)S(1)} %copy-done.3, s32[32]{0:T(128)S(1)} %copy-done.4, f32[576,1792]{1,0:T(8,128)} %bitcast.13, f32[576,1792]{1,0:T(8,128)} %bitcast.14), custom_call_target="tpu_custom_call" | custom-call | tf_op jit(solution)/shard_map/pallas_call | solution.py:478
  112.0 0.0 copy-start
  112.1 1.9 copy-done
  114.0 0.0 copy-start.1
  114.0 1.3 copy-done.1
  115.3 0.0 copy-start.2
  115.3 1.3 copy-done.2
  116.6 251.4 %shard_map.68 = (f32[576,1792]{1,0:T(8,128)}, bf16[576,1792]{1,0:T(8,128)(2,1)}, bf16[576,1792]{1,0:T(8,128)(2,1)}) custom-call(f32[576,1792]{1,0:T(8,128)} %copy-done, bf16[576,1792]{1,0:T(8,128)(2,1)} %copy-done.1, bf16[576,1792]{1,0:T(8,128)(2,1)} %copy-done.2), custom_call_target="tpu_custom_call" | custom-call | tf_op jit(solution)/shard_map/pallas_call | solution.py:516
Async XLA Ops:
  0.6 0.7 copy-start.3
  1.3 0.7 copy-start.4
  112.0 1.9 copy-start
  114.0 1.3 copy-start.1
  115.3 1.3 copy-start.2

commit v4 on v3

--- a/solution.py
+++ b/solution.py
@@ -19,10 +19,6 @@
 MAIN = 512
 OUT_PARTS = ((0, 256), (256, 768), (768, CDEV))
 WINDOW = 12
-PAIRS = ((0, 0), (2, 2), (1, 0), (0, 1), (3, 0), (0, 3), (2, 0), (0, 2),
-         (1, 2), (2, 1), (3, 2), (2, 3),
-         (1, 1), (3, 3), (1, 3), (3, 1))
-SLOTS = tuple((dy, dz, dc) for dy, dz in PAIRS for dc in (0, 1))
 GROUPS = (16, 24, 32)
 SHORT = 16 * GROUPS[0]
 TOPS = (SHORT + 64, 16 * GROUPS[1] + 64, ROWS)
@@ -39,43 +35,51 @@
     return lax.dot_general(a, b, (((1,), (1,)), ((), ())), preferred_element_type=F32)
 
 
+def away(n, group):
+    k, s = lax.rem(lax.div(n, 4), 4), lax.rem(lax.div(n, 2), 2)
+    if group == 0:
+        both = 2 * lax.div(3 - k, 3) * s
+        dy, dz = k * (1 - s) + both, k * s + both
+    elif group == 1:
+        odd = 1 + 2 * lax.rem(k, 2)
+        dy, dz = odd * (1 - s) + 2 * s, 2 * (1 - s) + odd * s
+    else:
+        dy, dz = 1 + 2 * s, 1 + 2 * lax.rem(s + k, 2)
+    return dy, dz, lax.rem(n, 2)
+
+
 def one_hot(match):
     return match.astype(F32).astype(BF16)
 
 
-def halving_places(ex, c):
-    near = ex + 1 - 2 * (ex % 2)
-    far = 3 - ex
-    first = (1 - c) * near + c * far
-    second = (1 - c) * far + c * near
-
-    def part(x):
-        h = (1 - c) * (((x + 1) // 2) % 2) + c * (x // 2)
-        q = (1 - c) * (x // 2) + c * (x % 2)
-        return h, q
-    return first, second, part
-
-
-def row_at(n):
-    return 16 * n + (64 if n >= GROUPS[0] else 0)
-
-
-def kernel(owner_s, cls_s, g_hbm, m_hbm, nm_hbm, up_hbm, own_hbm,
+def row_at(n, group):
+    return pl.multiple_of(16 * n + (64 if group else 0), 16)
+
+
+def kernel(owner_hbm, cls_hbm, g_hbm, m_hbm, nm_hbm, up_hbm, own_hbm,
            g, m, nm, zs, zmain, zlo, lor, x, ar1, ar2,
-           perm_m, perm_l, back_m, back_l, order, *rest):
-    sums = [rest[4 * i:4 * i + 4] for i in range(3)]
+           perm_m, perm_l, back_m, back_l, order, owner_s, cls_s, *rest):
+    sums = [rest[3 * i:3 * i + 3] for i in range(3)]
     (gram, t_ref, left, right, coef, u, ulo, vmain, vlo, vl, up, own,
-     in_sem, nm_sem, own_sem, up_sem, s1, r1, s2, r2, sm, rm, sl, rl, so, ro, slo, rlo, xs, xr) = rest[12:]
+     in_sem, nm_sem, own_sem, up_sem, s1, r1, s2, r2, sm, rm, sl, rl, so, ro, slo, rlo, xs, xr) = rest[9:]
     dp, ex = lax.axis_index("dp"), lax.axis_index("expert")
     y, z, c = dp // 8, (dp // 2) % 4, dp % 2
 
-    def ahead(n):
-        dy, dz, dc = SLOTS[n]
-        return (((y + dy) % 4) * 4 + (z + dz) % 4) * 2 + (c + dc) % 2
-
-    def behind(n):
-        dy, dz, dc = SLOTS[n]
-        return (((y + 4 - dy) % 4) * 4 + (z + 4 - dz) % 4) * 2 + (c + dc) % 2
+    def ahead(n, group):
+        dy, dz, dc = away(n, group)
+        return lax.rem(y + dy, 4) * 8 + lax.rem(z + dz, 4) * 2 + lax.rem(c + dc, 2)
+
+    def behind(n, group):
+        dy, dz, dc = away(n, group)
+        return lax.rem(y + 4 - dy, 4) * 8 + lax.rem(z + 4 - dz, 4) * 2 + lax.rem(c + dc, 2)
+
+    def each(lo, hi, act):
+        for group, (first, end) in enumerate(zip((0,) + GROUPS, GROUPS)):
+            if max(lo, first) < min(hi, end):
+                def step(n, _, group=group):
+                    act(n, group)
+                    return _
+                lax.fori_loop(max(lo, first), min(hi, end), step, 0)
 
     per = ROWS // LOADS
     loads = []
@@ -86,19 +90,22 @@
             cp.start()
             loads.append(cp)
 
+    tables = [pltpu.make_async_copy(src, dst, up_sem.at[i]) for i, (src, dst) in enumerate(((owner_hbm, owner_s), (cls_hbm, cls_s)))]
+    for cp in tables:
+        cp.start()
     barrier = pltpu.get_barrier_semaphore()
 
-    def greet(j, _):
-        to = (((y + j // 8) % 4) * 4 + (z + (j // 2) % 4) % 4) * 2 + (c + j % 2) % 2
-        pl.semaphore_signal(barrier, inc=1, device_id=(to, ex), device_id_type=MESH)
-        return _
-    lax.fori_loop(1, 32, greet, 0)
+    each(1, 32, lambda n, group: pl.semaphore_signal(
+        barrier, inc=1, device_id=(ahead(n, group), ex), device_id_type=MESH))
 
     def greet_x(j, _):
         zz, xx = (z + j % 4) % 4, (ex + j // 4) % 4
         pl.semaphore_signal(barrier, inc=1, device_id=((y * 4 + zz) * 2 + c, xx), device_id_type=MESH)
         return _
     lax.fori_loop(4, 16, greet_x, 0)
+
+    for cp in tables:
+        cp.wait()
 
     lane = lax.broadcasted_iota(jnp.int32, (8, ROWS), 1)
     mat = lax.broadcasted_iota(jnp.int32, (MATS, 128), 0)
@@ -184,8 +191,11 @@
     clip = jnp.minimum(1.0, jnp.sqrt(float(MATS * ROWS * COLS) / total))
     rate = (1.0 + MU_RATE) * clip
     sq = jnp.where(clip > 0.0, rate * rate * gg + 2.0 * rate * gm, 0.0) + mm
-    norm = jnp.sqrt(jnp.maximum(sq, 0.0))
-    inv = jnp.broadcast_to(1.0 / (norm + EPSILON), (MATS, 128))
+    bound = rate * rate * gg + mm
+    faint = jnp.where((clip > 0.0) & (sq < 1e-4 * bound), 1.0, 0.0)
+    sq = jnp.where(faint > 0.0, jnp.maximum(sq, 1e-7 * bound), sq)
+    divisor = jnp.sqrt(sq) + EPSILON
+    inv = jnp.broadcast_to(1.0 / divisor, (MATS, 128))
     clip = jnp.broadcast_to(clip, (MATS, 128))
 
     def blend(r, _):
@@ -208,32 +218,26 @@
     def block(ref, i):
         return ref.at[pl.ds(pl.multiple_of(i * 16, 16), 16)]
 
-    def slot(ref, n):
-        return ref.at[pl.ds(row_at(n), 16)]
-
-    def main_in(n):
-        to = ahead(n)
+    def slot(ref, n, group):
+        return ref.at[pl.ds(row_at(n, group), 16)]
+
+    def main_in(n, group):
+        to = ahead(n, group)
         return pltpu.make_async_remote_copy(
-            src_ref=block(zmain, to), dst_ref=slot(x, n), send_sem=sm.at[n], recv_sem=rm.at[n],
+            src_ref=block(zmain, to), dst_ref=slot(x, n, group), send_sem=sm.at[n], recv_sem=rm.at[n],
             device_id=(to, ex), device_id_type=MESH)
 
-    def lo_in(n):
-        to = ahead(n)
+    def lo_in(n, group):
+        to = ahead(n, group)
         return pltpu.make_async_remote_copy(
             src_ref=zlo.at[to], dst_ref=lor.at[n], send_sem=sl.at[n], recv_sem=rl.at[n],
             device_id=(to, ex), device_id_type=MESH)
 
-    def each(lo, hi, act):
-        for n in range(lo, hi):
-            act(n)
-
-    def go(n):
-        if n > WINDOW:
-            main_in(n - WINDOW).wait_send()
-        main_in(n).start()
-
-    each(1, 32, lambda n: lo_in(n).start())
-    each(1, WINDOW + 1, go)
+    def sent(lo, hi):
+        each(lo, hi, lambda n, group: main_in(n, group).wait_send())
+
+    each(1, 32, lambda n, group: lo_in(n, group).start())
+    each(1, WINDOW + 1, lambda n, group: main_in(n, group).start())
     save_nm = pltpu.make_async_copy(nm, nm_hbm, nm_sem)
     save_nm.start()
     x[0:16, :] = zmain[pl.ds(pl.multiple_of(dp * 16, 16), 16), :]
@@ -243,6 +247,9 @@
     mats = lax.broadcasted_iota(jnp.int32, (MATS, MAIN), 0)
     for i in range(MATS):
         owner_col = jnp.where(mats == i, owner_s[i], owner_col)
+    here = owner_col[:, :1] == dp
+    divisor = jnp.sum(jnp.where(here, divisor, 0.0), axis=0, keepdims=True)
+    faint = jnp.sum(jnp.where(here, faint, 0.0), axis=0, keepdims=True)
     owner_col = owner_col * RDEV
     key = ((lane // 16) * RDEV + lane % 16)[0:1, :MAIN]
     for r in range(16):
@@ -252,21 +259,23 @@
         back_l[MATS * r:MATS * (r + 1), :] = one_hot(owner_col[:, :64] + (16 + r) == key)
     short = (lane >= SHORT) & (lane < SHORT + 64)
     n = jnp.where(short, (lane - SHORT) // 2, jnp.where(lane < SHORT, lane // 16, lane // 16 - 4))
-    source = jnp.zeros((8, ROWS), jnp.int32)
-    for k in range(32):
-        source = jnp.where(n == k, behind(k), source)
+    source = jnp.where(n < GROUPS[0], behind(n, 0), jnp.where(n < GROUPS[1], behind(n, 1), behind(n, 2)))
     key = (source * RDEV + jnp.where(short, 16 + lane % 2, lane % 16))[0:1]
     for k in range(RDEV):
         rows = lax.broadcasted_iota(jnp.int32, (MATS, ROWS), 0) + MATS * k
         order[MATS * k:MATS * (k + 1), :] = one_hot(rows == key)
 
+    def go(n, group):
+        early = n - WINDOW
+        main_in(early, 0).wait_send()
+        main_in(n, group).start()
     each(WINDOW + 1, GROUPS[0] + WINDOW, go)
 
     def arrive(ref_at, sem, n):
         pltpu.make_async_copy(ref_at, ref_at, sem.at[n]).wait()
 
-    each(1, GROUPS[0], lambda n: arrive(slot(x, n), rm, n))
-    each(1, 32, lambda n: arrive(lor.at[n], rl, n))
+    each(1, GROUPS[0], lambda n, group: arrive(slot(x, n, group), rm, n))
+    each(1, 32, lambda n, group: arrive(lor.at[n], rl, n))
     x[SHORT:SHORT + 64, :] = lor[...].astype(F32).reshape(64, CDEV).astype(BF16)
 
     def put(part, n, piece):
@@ -287,57 +296,38 @@
         for n in range(2 * len(PANELS[i]), 4 * QUARTERS[i]):
             part[n] = jnp.zeros((32, 128), F32)
 
-    first, second, part_of = halving_places(ex, c)
-    h, q = part_of(ex)
-    h1, q1 = part_of(first)
-
     class Sum:
-        def __init__(self, part, got_a, got_b, full, size, base):
-            self.part, self.got_a, self.got_b, self.full, self.size, self.base = part, got_a, got_b, full, size, base
-
-        def at(self, hh, qq):
-            return pl.ds((2 * hh + qq) * self.size, self.size)
-
-        def move(self, src, dst, n, to):
+        def __init__(self, part, got, full, size, base):
+            self.part, self.got, self.full, self.size, self.base = part, got, full, size, base
+
+        def at(self, xx):
+            return pl.ds(xx * self.size, self.size)
+
+        def move(self, src, dst, n, far):
             return pltpu.make_async_remote_copy(
                 src_ref=src, dst_ref=dst, send_sem=xs.at[self.base + n], recv_sem=xr.at[self.base + n],
-                device_id=(dp, to), device_id_type=MESH)
-
-        def halves(self):
-            self.a1 = self.move(self.part.at[self.at(h1, 1 - q1)], self.got_a.at[0], 0, first)
-            self.a2 = self.move(self.part.at[self.at(h1, q1)], self.got_a.at[1], 1, first)
-            self.a1.start()
-            self.a2.start()
-
-        def quarters(self):
-            self.a1.wait_recv()
-            pass_on = self.at(h, 1 - q)
-            self.part[pass_on] = self.part[pass_on] + self.got_a[0]
-            self.b = self.move(self.part.at[pass_on], self.got_b, 2, second)
-            self.b.start()
-
-        def finish(self):
-            self.a2.wait_recv()
-            self.b.wait_recv()
-            keep = self.at(h, q)
-            self.full[keep] = self.part[keep] + self.got_a[1] + self.got_b[...]
-            self.c1 = self.move(self.full.at[keep], self.full.at[keep], 3, second)
-            self.c2 = self.move(self.full.at[keep], self.full.at[keep], 4, first)
-            self.c1.start()
-            self.c2.start()
-
-        def forward(self):
-            self.c1.wait_recv()
-            other = self.at(h, 1 - q)
-            self.c3 = self.move(self.full.at[other], self.full.at[other], 5, first)
-            self.c3.start()
+                device_id=(dp, (ex + far) % 4), device_id_type=MESH)
+
+        def scatter(self):
+            self.out = [self.move(self.part.at[self.at((ex + far) % 4)], self.got.at[far - 1], far - 1, far) for far in (2, 1, 3)]
+            for cp in self.out:
+                cp.start()
+
+        def reduce(self):
+            for cp in self.out:
+                cp.wait_recv()
+            here = self.full.at[self.at(ex)]
+            self.full[self.at(ex)] = self.part[self.at(ex)] + self.got[0] + (self.got[1] + self.got[2])
+            self.back = [self.move(here, here, 2 + far, far) for far in (2, 1, 3)]
+            for cp in self.back:
+                cp.start()
 
         def done(self):
-            self.c2.wait_recv()
-            self.c3.wait_recv()
+            for cp in self.back:
+                cp.wait_recv()
 
         def sent(self):
-            for cp in (self.a1, self.a2, self.b, self.c1, self.c2, self.c3):
+            for cp in self.out + self.back:
                 cp.wait_send()
 
     def lay_out(i, full):
@@ -352,29 +342,45 @@
 
     e1, e2, e3 = (Sum(*sums[i], QUARTERS[i], 6 * i) for i in range(3))
     terms(0, e1.part)
-    e1.halves()
-    each(GROUPS[0] + WINDOW, 32, go)
-    e1.quarters()
-    each(GROUPS[0], GROUPS[1], lambda n: arrive(slot(x, n), rm, n))
+    e1.scatter()
+
+    def rest_go(n, group):
+        main_in(n - WINDOW, 1).wait_send()
+        main_in(n, group).start()
+    each(GROUPS[0] + WINDOW, 32, rest_go)
+    e1.reduce()
+    each(GROUPS[0], GROUPS[1], lambda n, group: arrive(slot(x, n, group), rm, n))
     terms(1, e2.part)
-    e2.halves()
-    e1.finish()
-    e2.quarters()
-    e1.forward()
-    each(GROUPS[1], 32, lambda n: arrive(slot(x, n), rm, n))
-    terms(2, e3.part)
-    e3.halves()
-    e2.finish()
+    e2.scatter()
     e1.done()
     lay_out(0, e1.full)
-    e2.forward()
-    e3.quarters()
+    e2.reduce()
+    each(GROUPS[1], 32, lambda n, group: arrive(slot(x, n, group), rm, n))
+    terms(2, e3.part)
+    e3.scatter()
     e2.done()
     lay_out(1, e2.full)
-    e3.finish()
-    e3.forward()
+    e3.reduce()
     e3.done()
     lay_out(2, e3.full)
+
+    def symmetric(out, a, b, more=None):
+        head = dot(a, b[:, :MAIN])
+        corner = dot(a[MAIN:, :], b[:, MAIN:])
+        if more is not None:
+            head = head + COEF_A * more[:, :MAIN]
+            corner = corner + COEF_A * more[MAIN:, MAIN:]
+        out[:, :MAIN] = head
+        out[MAIN:, MAIN:] = corner
+        out[:MAIN, MAIN:] = out[MAIN:, :MAIN].T
+
+    diagonal = lax.broadcasted_iota(jnp.int32, (64, 64), 0) == lax.broadcasted_iota(jnp.int32, (64, 64), 1)
+    trace = jnp.zeros((64, 64), F32)
+    for r in range(ROWS // 64):
+        trace = trace + jnp.where(diagonal, gram[64 * r:64 * r + 64, 64 * r:64 * r + 64], 0.0)
+    trace = jnp.sum(jnp.sum(trace, axis=1, keepdims=True), axis=0, keepdims=True)
+    fit = jnp.where(faint > 0.0, divisor / (jnp.sqrt(trace) * divisor + EPSILON), 1.0)
+    gram[...] = gram[...] * (fit * fit)
 
     left[:, ROWS:640] = jnp.zeros((ROWS, 64), BF16)
     left[:, 640 + ROWS:] = jnp.zeros((ROWS, 64), BF16)
@@ -382,10 +388,11 @@
     right[640 + ROWS:, :] = jnp.zeros((64, ROWS), BF16)
     for k in range(ITERS):
         a16 = gram[...].astype(BF16)
-        b16 = (COEF_B * a16.astype(F32) + COEF_C * dot(a16, a16)).astype(BF16)
+        left[:, :ROWS] = a16
+        symmetric(t_ref, left[:, :ROWS], a16)
+        b16 = (COEF_B * a16.astype(F32) + COEF_C * t_ref[...]).astype(BF16)
         coef[k] = b16
         if k + 1 < ITERS:
-            left[:, :ROWS] = a16
             left[:, 640:640 + ROWS] = (gram[...] - a16.astype(F32)).astype(BF16)
             right[:ROWS, :] = b16
             right[640:640 + ROWS, :] = b16
@@ -395,18 +402,18 @@
             t16 = t_ref[...].astype(BF16)
             right[:ROWS, :] = t16
             right[640:640 + ROWS, :] = (t_ref[...] - t16.astype(F32)).astype(BF16)
-            gram[...] = COEF_A * t_ref[...] + dot(left[...], right[...])
-
-    def main_out(p, n):
-        to = behind(n)
+            symmetric(gram, left[...], right[...], t_ref)
+
+    def main_out(p, n, group):
+        to = behind(n, group)
         cols = pl.ds(OUT_PARTS[p][0], OUT_PARTS[p][1] - OUT_PARTS[p][0])
         return pltpu.make_async_remote_copy(
-            src_ref=u.at[pl.ds(row_at(n), 16), cols],
+            src_ref=u.at[pl.ds(row_at(n, group), 16), cols],
             dst_ref=vmain.at[pl.ds(pl.multiple_of(dp * 16, 16), 16), cols],
             send_sem=so.at[p, n], recv_sem=ro.at[p, n], device_id=(to, ex), device_id_type=MESH)
 
-    def lo_out(n):
-        to = behind(n)
+    def lo_out(n, group):
+        to = behind(n, group)
         return pltpu.make_async_remote_copy(
             src_ref=ulo.at[n], dst_ref=vlo.at[dp], send_sem=slo.at[n], recv_sem=rlo.at[n],
             device_id=(to, ex), device_id_type=MESH)
@@ -417,13 +424,15 @@
             cur = x[:, cols]
             for k in range(ITERS):
                 out = COEF_A * cur.astype(F32) + dot(coef[k], cur)
+                if k == 0:
+                    out = out * fit
                 if k + 1 < ITERS:
                     cur = out.astype(BF16)
             res = (SCALE * out).astype(BF16)
             u[:, cols] = res
             ulo[:, :, cols] = res[SHORT:SHORT + 64].astype(F32).reshape(MATS, 2, cols.stop - at).astype(BF16)
-        each(1, 32, lambda n, p=p: main_out(p, n).start())
-    each(1, 32, lambda n: lo_out(n).start())
+        each(1, 32, lambda n, group, p=p: main_out(p, n, group).start())
+    each(1, 32, lambda n, group: lo_out(n, group).start())
 
     vmain[pl.ds(pl.multiple_of(dp * 16, 16), 16), :] = u[0:16, :]
     vlo[dp] = ulo[0]
@@ -437,8 +446,8 @@
     for p, (lo, hi) in enumerate(OUT_PARTS):
         part_cols = pl.ds(lo, hi - lo)
 
-        def landed(n, p=p, part_cols=part_cols):
-            at = vmain.at[pl.ds(pl.multiple_of(ahead(n) * 16, 16), 16), part_cols]
+        def landed(n, group, p=p, part_cols=part_cols):
+            at = vmain.at[pl.ds(pl.multiple_of(ahead(n, group) * 16, 16), 16), part_cols]
             pltpu.make_async_copy(at, at, ro.at[p, n]).wait()
         each(1, 32, landed)
         for at in range(lo, hi, 256):
@@ -447,7 +456,7 @@
         cp = pltpu.make_async_copy(up.at[pl.ds(0, MAIN), part_cols], up_hbm.at[pl.ds(0, MAIN), part_cols], up_sem.at[p])
         cp.start()
         saves.append(cp)
-    each(1, 32, lambda n: arrive(vlo.at[ahead(n)], rlo, n))
+    each(1, 32, lambda n, group: arrive(vlo.at[ahead(n, group)], rlo, n))
     vl[...] = vlo[...].astype(F32).reshape(64, CDEV).astype(BF16)
     up[MAIN:, :] = dot(back_l[...], vl[...]).astype(BF16)
     cp = pltpu.make_async_copy(up.at[pl.ds(MAIN, 64)], up_hbm.at[pl.ds(MAIN, 64)], up_sem.at[len(OUT_PARTS)])
@@ -458,13 +467,13 @@
         one(j).wait_send()
     for j in range(1, 16):
         two(j).wait_send()
-    each(1, 32, lambda n: lo_in(n).wait_send())
-    each(32 - WINDOW, 32, lambda n: main_in(n).wait_send())
+    each(1, 32, lambda n, group: lo_in(n, group).wait_send())
+    sent(32 - WINDOW, 32)
     for e in (e1, e2, e3):
         e.sent()
     for p in range(len(OUT_PARTS)):
-        each(1, 32, lambda n, p=p: main_out(p, n).wait_send())
-    each(1, 32, lambda n: lo_out(n).wait_send())
+        each(1, 32, lambda n, group, p=p: main_out(p, n, group).wait_send())
+    each(1, 32, lambda n, group: lo_out(n, group).wait_send())
     save_nm.wait()
     save_own.wait()
     for cp in saves:
@@ -478,14 +487,15 @@
     return pl.pallas_call(
         kernel,
         out_shape=(jax.ShapeDtypeStruct(wide, F32), jax.ShapeDtypeStruct(wide, BF16), jax.ShapeDtypeStruct(wide, BF16)),
-        in_specs=[pl.BlockSpec(memory_space=pltpu.SMEM)] * 2 + [pl.BlockSpec(memory_space=pl.ANY)] * 2,
+        in_specs=[pl.BlockSpec(memory_space=pltpu.HBM)] * 4,
         out_specs=(pl.BlockSpec(memory_space=pl.ANY),) * 3,
         scratch_shapes=[
             V(wide, F32), V(wide, F32), V(wide, F32), V(wide, BF16),
             V((MAIN, CDEV), BF16), V((MATS, 2, CDEV), BF16), V((MATS, 2, CDEV), BF16), V(wide, BF16),
             V((8, 8, 128), F32), V((16, 8, 128), F32),
             V((MAIN, MAIN), BF16), V((64, 64), BF16), V((MAIN, MAIN), BF16), V((64, 64), BF16), V(square, BF16),
-            *[V((k * q, 32, 128), F32) if k else V((2, q, 32, 128), F32) for q in QUARTERS for k in (4, 0, 1, 4)],
+            pltpu.SMEM((MATS,), jnp.int32), pltpu.SMEM((MATS,), jnp.int32),
+            *[V(shape, F32) for q in QUARTERS for shape in ((4 * q, 32, 128), (3, q, 32, 128), (4 * q, 32, 128))],
             V(square, F32), V(square, F32), V((ROWS, 1280), BF16), V((1280, ROWS), BF16), V((ITERS, ROWS, ROWS), BF16),
             V(wide, BF16), V((MATS, 2, CDEV), BF16), V((MAIN, CDEV), BF16), V((MATS, 2, CDEV), BF16), V((64, CDEV), BF16),
             V(wide, BF16), V(wide, BF16),
@@ -497,35 +507,10 @@
     )(owner, cls, g, m)
 
 
-PIECES = 4
-
-
-def place_kernel(*refs):
-    copies = []
-    for i in range(3):
-        for k in range(PIECES):
-            rows = pl.ds(k * (ROWS // PIECES), ROWS // PIECES)
-            copies.append(pltpu.make_async_copy(refs[i].at[rows], refs[3 + i].at[rows], refs[6].at[i, k]))
-    for cp in copies:
-        cp.start()
-    for cp in copies:
-        cp.wait()
-
-
-def placed(*arrays):
-    return pl.pallas_call(
-        place_kernel,
-        out_shape=tuple(jax.ShapeDtypeStruct(a.shape, a.dtype) for a in arrays),
-        in_specs=[pl.BlockSpec(memory_space=pl.ANY)] * 3,
-        out_specs=(pl.BlockSpec(memory_space=pl.ANY),) * 3,
-        scratch_shapes=[pltpu.SemaphoreType.DMA((3, PIECES))],
-    )(*arrays)
-
-
 def body(gradient, momentum, owner_table, shape_class):
     g = jnp.transpose(gradient, (1, 0, 2)).reshape(ROWS, CDEV)
     m = jnp.transpose(momentum, (1, 0, 2)).reshape(ROWS, CDEV)
-    nm, up, own = placed(*step(owner_table, shape_class, g, m))
+    nm, up, own = step(owner_table, shape_class, g, m)
     new_moment = jnp.transpose(nm.reshape(RDEV, MATS, CDEV), (1, 0, 2))
     update = jnp.transpose(up.reshape(RDEV, MATS, CDEV), (1, 0, 2))
     return new_moment, update, own[None]

time: 369 us -> 122 us (0.33)
  Pallas kernels: 361 us -> 115 us
    pallas_call x1 -> x0, Pallas kernels: 251 us -> none  [placed(): pl.pallas_call(place_kernel, out_shape=tuple((jax.ShapeDtypeStruct(a.shap...]
    pallas_call x1, Pallas kernels: 110 us -> 115 us  [step(): pl.pallas_call(kernel, out_shape=(jax.ShapeDtypeStruct(wide, F32), jax.Sh...]
where the time goes in v4:
time: 122 us; the launch traced here: 121 us
  Pallas kernels  115 us (94%)
  local copies, waits for them, and re-layouts  5.9 us (5%)
    pallas_call x1, Pallas kernels, step(): pl.pallas_call(kernel, out_shape=(jax.ShapeDtypeStruct(wide, F32), jax.Sh...  115 us
    unnamed x7, local copies, waits for them, and re-layouts  5.9 us

profile of v4, /device:TPU:1, one launch (start us, length us, event | category | flops | bytes accessed | tf_op | source)
XLA Modules:
  0.0 121.1 jit_solution(13243972856831084878)
XLA Ops:
  0.6 0.0 copy-start
  0.6 0.6 copy-done
  1.3 0.0 copy-start.1
  1.3 0.7 copy-done.1
  1.9 114.5 %shard_map.67 = (f32[576,1792]{1,0:T(8,128)S(1)}, bf16[576,1792]{1,0:T(8,128)(2,1)S(1)}, bf16[576,1792]{1,0:T(8,128)(2,1)S(1)}) custom-call(s32[32]{0:T(128)S(1)} %copy-done, s32[32]{0:T(128)S(1)} %copy-done.1, f32[576,1792]{1,0:T(8,128)} %bitcast.16, f32[576,1792]{1,0:T(8,128)} %bitcast.17), custom_call_target="tpu_custom_call" | custom-call | tf_op jit(solution)/shard_map/pallas_call | solution.py:487
  116.5 2.0 %copy.10 = f32[32,18,1792]{2,0,1:T(8,128)} copy(f32[32,18,1792]{2,0,1:T(8,128)S(1)} %bitcast.13) | data formatting | bytes 8257536
  118.4 1.3 %copy.11 = bf16[32,18,1792]{2,0,1:T(8,128)(2,1)} copy(bf16[32,18,1792]{2,0,1:T(8,128)(2,1)S(1)} %bitcast.15) | data formatting | bytes 4128768
  119.8 1.3 %copy.12 = bf16[1,576,1792]{2,1,0:T(8,128)(2,1)} copy(bf16[1,576,1792]{2,1,0:T(8,128)(2,1)S(1)} %bitcast.14) | data formatting | bytes 4128768
Async XLA Ops:
  0.6 0.7 copy-start
  1.3 0.7 copy-start.1

commit v5 on v4

--- a/solution.py
+++ b/solution.py
@@ -99,7 +99,7 @@
         barrier, inc=1, device_id=(ahead(n, group), ex), device_id_type=MESH))
 
     def greet_x(j, _):
-        zz, xx = (z + j % 4) % 4, (ex + j // 4) % 4
+        zz, xx = lax.rem(z + lax.rem(j, 4), 4), lax.rem(ex + lax.div(j, 4), 4)
         pl.semaphore_signal(barrier, inc=1, device_id=((y * 4 + zz) * 2 + c, xx), device_id_type=MESH)
         return _
     lax.fori_loop(4, 16, greet_x, 0)
@@ -157,7 +157,7 @@
         return pltpu.make_async_copy(buf.at[slot], buf.at[slot], sem.at[slot])
 
     def one_of(j):
-        return (y + j // 2) % 4, (c + j % 2) % 2
+        return lax.rem(y + j // 2, 4), lax.rem(c + j % 2, 2)
 
     def one(j):
         yy, cc = one_of(j)
@@ -166,7 +166,7 @@
             device_id=((yy * 4 + z) * 2 + cc, ex), device_id_type=MESH)
 
     def two_of(j):
-        return (z + j % 4) % 4, (ex + j // 4) % 4
+        return lax.rem(z + j % 4, 4), lax.rem(ex + j // 4, 4)
 
     def two(j):
         zz, xx = two_of(j)
@@ -224,17 +224,14 @@
     def main_in(n, group):
         to = ahead(n, group)
         return pltpu.make_async_remote_copy(
-            src_ref=block(zmain, to), dst_ref=slot(x, n, group), send_sem=sm.at[n], recv_sem=rm.at[n],
+            src_ref=block(zmain, to), dst_ref=slot(x, n, group), send_sem=sm.at[n], recv_sem=rm.at[group],
             device_id=(to, ex), device_id_type=MESH)
 
     def lo_in(n, group):
         to = ahead(n, group)
         return pltpu.make_async_remote_copy(
-            src_ref=zlo.at[to], dst_ref=lor.at[n], send_sem=sl.at[n], recv_sem=rl.at[n],
+            src_ref=zlo.at[to], dst_ref=lor.at[n], send_sem=sl.at[0], recv_sem=rl.at[0],
             device_id=(to, ex), device_id_type=MESH)
-
-    def sent(lo, hi):
-        each(lo, hi, lambda n, group: main_in(n, group).wait_send())
 
     each(1, 32, lambda n, group: lo_in(n, group).start())
     each(1, WINDOW + 1, lambda n, group: main_in(n, group).start())
@@ -271,11 +268,11 @@
         main_in(n, group).start()
     each(WINDOW + 1, GROUPS[0] + WINDOW, go)
 
-    def arrive(ref_at, sem, n):
+    def all_of(ref_at, sem, n=0):
         pltpu.make_async_copy(ref_at, ref_at, sem.at[n]).wait()
 
-    each(1, GROUPS[0], lambda n, group: arrive(slot(x, n, group), rm, n))
-    each(1, 32, lambda n, group: arrive(lor.at[n], rl, n))
+    all_of(x.at[pl.ds(16, SHORT - 16)], rm, 0)
+    all_of(lor.at[pl.ds(1, MATS - 1)], rl)
     x[SHORT:SHORT + 64, :] = lor[...].astype(F32).reshape(64, CDEV).astype(BF16)
 
     def put(part, n, piece):
@@ -348,19 +345,19 @@
         main_in(n - WINDOW, 1).wait_send()
         main_in(n, group).start()
     each(GROUPS[0] + WINDOW, 32, rest_go)
-    e1.reduce()
-    each(GROUPS[0], GROUPS[1], lambda n, group: arrive(slot(x, n, group), rm, n))
+    all_of(x.at[pl.ds(TOPS[0], TOPS[1] - TOPS[0])], rm, 1)
     terms(1, e2.part)
     e2.scatter()
+    e1.reduce()
+    all_of(x.at[pl.ds(TOPS[1], TOPS[2] - TOPS[1])], rm, 2)
+    terms(2, e3.part)
+    e3.scatter()
+    e2.reduce()
     e1.done()
     lay_out(0, e1.full)
-    e2.reduce()
-    each(GROUPS[1], 32, lambda n, group: arrive(slot(x, n, group), rm, n))
-    terms(2, e3.part)
-    e3.scatter()
+    e3.reduce()
     e2.done()
     lay_out(1, e2.full)
-    e3.reduce()
     e3.done()
     lay_out(2, e3.full)
 
@@ -410,12 +407,12 @@
         return pltpu.make_async_remote_copy(
             src_ref=u.at[pl.ds(row_at(n, group), 16), cols],
             dst_ref=vmain.at[pl.ds(pl.multiple_of(dp * 16, 16), 16), cols],
-            send_sem=so.at[p, n], recv_sem=ro.at[p, n], device_id=(to, ex), device_id_type=MESH)
+            send_sem=so.at[p], recv_sem=ro.at[p], device_id=(to, ex), device_id_type=MESH)
 
     def lo_out(n, group):
         to = behind(n, group)
         return pltpu.make_async_remote_copy(
-            src_ref=ulo.at[n], dst_ref=vlo.at[dp], send_sem=slo.at[n], recv_sem=rlo.at[n],
+            src_ref=ulo.at[n], dst_ref=vlo.at[dp], send_sem=slo.at[0], recv_sem=rlo.at[0],
             device_id=(to, ex), device_id_type=MESH)
 
     for p, (lo, hi) in enumerate(OUT_PARTS):
@@ -442,39 +439,36 @@
     save_own = pltpu.make_async_copy(own, own_hbm, own_sem)
     save_own.start()
 
+    for j in range(1, 8):
+        one(j).wait_send()
+    for j in range(1, 16):
+        two(j).wait_send()
+    all_of(zlo.at[pl.ds(0, MATS - 1)], sl)
+    each(32 - WINDOW, 32, lambda n, group: main_in(n, group).wait_send())
+    for e in (e1, e2, e3):
+        e.sent()
+    save_nm.wait()
+
     saves = []
     for p, (lo, hi) in enumerate(OUT_PARTS):
         part_cols = pl.ds(lo, hi - lo)
-
-        def landed(n, group, p=p, part_cols=part_cols):
-            at = vmain.at[pl.ds(pl.multiple_of(ahead(n, group) * 16, 16), 16), part_cols]
-            pltpu.make_async_copy(at, at, ro.at[p, n]).wait()
-        each(1, 32, landed)
+        all_of(vmain.at[pl.ds(0, MAIN - 16), part_cols], ro, p)
         for at in range(lo, hi, 256):
             cols = slice(at, at + 256)
             up[:MAIN, cols] = dot(back_m[...], vmain[:, cols]).astype(BF16)
         cp = pltpu.make_async_copy(up.at[pl.ds(0, MAIN), part_cols], up_hbm.at[pl.ds(0, MAIN), part_cols], up_sem.at[p])
         cp.start()
         saves.append(cp)
-    each(1, 32, lambda n, group: arrive(vlo.at[ahead(n, group)], rlo, n))
+    all_of(vlo.at[pl.ds(0, MATS - 1)], rlo)
     vl[...] = vlo[...].astype(F32).reshape(64, CDEV).astype(BF16)
     up[MAIN:, :] = dot(back_l[...], vl[...]).astype(BF16)
     cp = pltpu.make_async_copy(up.at[pl.ds(MAIN, 64)], up_hbm.at[pl.ds(MAIN, 64)], up_sem.at[len(OUT_PARTS)])
     cp.start()
     saves.append(cp)
 
-    for j in range(1, 8):
-        one(j).wait_send()
-    for j in range(1, 16):
-        two(j).wait_send()
-    each(1, 32, lambda n, group: lo_in(n, group).wait_send())
-    sent(32 - WINDOW, 32)
-    for e in (e1, e2, e3):
-        e.sent()
-    for p in range(len(OUT_PARTS)):
-        each(1, 32, lambda n, group, p=p: main_out(p, n, group).wait_send())
-    each(1, 32, lambda n, group: lo_out(n, group).wait_send())
-    save_nm.wait()
+    for p, (lo, hi) in enumerate(OUT_PARTS):
+        all_of(u.at[pl.ds(0, MAIN - 16), pl.ds(lo, hi - lo)], so, p)
+    all_of(ulo.at[pl.ds(0, MATS - 1)], slo)
     save_own.wait()
     for cp in saves:
         cp.wait()
@@ -500,8 +494,8 @@
             V(wide, BF16), V((MATS, 2, CDEV), BF16), V((MAIN, CDEV), BF16), V((MATS, 2, CDEV), BF16), V((64, CDEV), BF16),
             V(wide, BF16), V(wide, BF16),
             D((2, LOADS)), D, D, D((len(OUT_PARTS) + 1,)),
-            D((8,)), D((8,)), D((16,)), D((16,)), D((32,)), D((32,)), D((32,)), D((32,)),
-            D((len(OUT_PARTS), 32)), D((len(OUT_PARTS), 32)), D((32,)), D((32,)), D((18,)), D((18,)),
+            D((8,)), D((8,)), D((16,)), D((16,)), D((32,)), D((len(GROUPS),)), D((1,)), D((1,)),
+            D((len(OUT_PARTS),)), D((len(OUT_PARTS),)), D((1,)), D((1,)), D((18,)), D((18,)),
         ],
         compiler_params=pltpu.CompilerParams(collective_id=0, has_side_effects=True, vmem_limit_bytes=VMEM_LIMIT),
     )(owner, cls, g, m)

time: 122 us -> 109 us (0.89)
  Pallas kernels: 115 us -> 103 us
    pallas_call x1, Pallas kernels: 115 us -> 103 us  [step(): pl.pallas_call(kernel, out_shape=(jax.ShapeDtypeStruct(wide, F32), jax.Sh...]
where the time goes in v5:
time: 109 us
  Pallas kernels  103 us (94%)
  local copies, waits for them, and re-layouts  5.9 us (5%)
    pallas_call x1, Pallas kernels, step(): pl.pallas_call(kernel, out_shape=(jax.ShapeDtypeStruct(wide, F32), jax.Sh...  103 us
    unnamed x7, local copies, waits for them, and re-layouts  5.9 us

profile of v5, /device:TPU:1, one launch (start us, length us, event | category | flops | bytes accessed | tf_op | source)
XLA Modules:
  0.0 109.2 jit_solution(4985090937868890152)
XLA Ops:
  0.6 0.0 copy-start
  0.6 0.6 copy-done
  1.3 0.0 copy-start.1
  1.3 0.7 copy-done.1
  1.9 102.6 %shard_map.67 = (f32[576,1792]{1,0:T(8,128)S(1)}, bf16[576,1792]{1,0:T(8,128)(2,1)S(1)}, bf16[576,1792]{1,0:T(8,128)(2,1)S(1)}) custom-call(s32[32]{0:T(128)S(1)} %copy-done, s32[32]{0:T(128)S(1)} %copy-done.1, f32[576,1792]{1,0:T(8,128)} %bitcast.16, f32[576,1792]{1,0:T(8,128)} %bitcast.17), custom_call_target="tpu_custom_call" | custom-call | tf_op jit(solution)/shard_map/pallas_call | solution.py:481
  104.6 2.0 %copy.10 = f32[32,18,1792]{2,0,1:T(8,128)} copy(f32[32,18,1792]{2,0,1:T(8,128)S(1)} %bitcast.13) | data formatting | bytes 8257536
  106.6 1.3 %copy.11 = bf16[32,18,1792]{2,0,1:T(8,128)(2,1)} copy(bf16[32,18,1792]{2,0,1:T(8,128)(2,1)S(1)} %bitcast.15) | data formatting | bytes 4128768
  107.9 1.3 %copy.12 = bf16[1,576,1792]{2,1,0:T(8,128)(2,1)} copy(bf16[1,576,1792]{2,1,0:T(8,128)(2,1)S(1)} %bitcast.14) | data formatting | bytes 4128768
Async XLA Ops:
  0.6 0.7 copy-start
  1.3 0.7 copy-start.1

commit v6 on v5

--- a/solution.py
+++ b/solution.py
@@ -81,6 +81,16 @@
                     return _
                 lax.fori_loop(max(lo, first), min(hi, end), step, 0)
 
+    barrier = pltpu.get_barrier_semaphore()
+    each(1, 32, lambda n, group: pl.semaphore_signal(
+        barrier, inc=1, device_id=(ahead(n, group), ex), device_id_type=MESH))
+
+    def greet_x(j, _):
+        zz, xx = lax.rem(z + lax.rem(j, 4), 4), lax.rem(ex + lax.div(j, 4), 4)
+        pl.semaphore_signal(barrier, inc=1, device_id=((y * 4 + zz) * 2 + c, xx), device_id_type=MESH)
+        return _
+    lax.fori_loop(4, 16, greet_x, 0)
+
     per = ROWS // LOADS
     loads = []
     for k in range(LOADS):
@@ -89,20 +99,9 @@
             cp = pltpu.make_async_copy(src.at[rows], dst.at[rows], in_sem.at[n, k])
             cp.start()
             loads.append(cp)
-
     tables = [pltpu.make_async_copy(src, dst, up_sem.at[i]) for i, (src, dst) in enumerate(((owner_hbm, owner_s), (cls_hbm, cls_s)))]
     for cp in tables:
         cp.start()
-    barrier = pltpu.get_barrier_semaphore()
-
-    each(1, 32, lambda n, group: pl.semaphore_signal(
-        barrier, inc=1, device_id=(ahead(n, group), ex), device_id_type=MESH))
-
-    def greet_x(j, _):
-        zz, xx = lax.rem(z + lax.rem(j, 4), 4), lax.rem(ex + lax.div(j, 4), 4)
-        pl.semaphore_signal(barrier, inc=1, device_id=((y * 4 + zz) * 2 + c, xx), device_id_type=MESH)
-        return _
-    lax.fori_loop(4, 16, greet_x, 0)
 
     for cp in tables:
         cp.wait()
@@ -153,8 +152,8 @@
     i1, i2 = y * 2 + c, ex * 4 + z
     ar1[i1] = mine
 
-    def got(buf, slot, sem):
-        return pltpu.make_async_copy(buf.at[slot], buf.at[slot], sem.at[slot])
+    def all_of(ref_at, sem, n=0):
+        pltpu.make_async_copy(ref_at, ref_at, sem.at[n]).wait()
 
     def one_of(j):
         return lax.rem(y + j // 2, 4), lax.rem(c + j % 2, 2)
@@ -162,7 +161,7 @@
     def one(j):
         yy, cc = one_of(j)
         return pltpu.make_async_remote_copy(
-            src_ref=ar1.at[i1], dst_ref=ar1.at[i1], send_sem=s1.at[j], recv_sem=r1.at[i1],
+            src_ref=ar1.at[i1], dst_ref=ar1.at[i1], send_sem=s1.at[j], recv_sem=r1.at[0],
             device_id=((yy * 4 + z) * 2 + cc, ex), device_id_type=MESH)
 
     def two_of(j):
@@ -171,20 +170,16 @@
     def two(j):
         zz, xx = two_of(j)
         return pltpu.make_async_remote_copy(
-            src_ref=ar2.at[i2], dst_ref=ar2.at[i2], send_sem=s2.at[j], recv_sem=r2.at[i2],
+            src_ref=ar2.at[i2], dst_ref=ar2.at[i2], send_sem=s2.at[j], recv_sem=r2.at[0],
             device_id=((y * 4 + zz) * 2 + c, xx), device_id_type=MESH)
 
     for j in range(1, 8):
         one(j).start()
-    for j in range(1, 8):
-        yy, cc = one_of(j)
-        got(ar1, yy * 2 + cc, r1).wait()
+    all_of(ar1.at[pl.ds(0, 7)], r1)
     ar2[i2] = jnp.sum(ar1[...], axis=0)
     for j in range(1, 16):
         two(j).start()
-    for j in range(1, 16):
-        zz, xx = two_of(j)
-        got(ar2, xx * 4 + zz, r2).wait()
+    all_of(ar2.at[pl.ds(0, 15)], r2)
     tot = jnp.concatenate([jnp.sum(ar2[...], axis=0), jnp.zeros((120, 128), F32)], axis=0).T[:MATS]
     gg, gm, mm = tot[:, 0:1], tot[:, 1:2], tot[:, 2:3]
     total = jnp.sum(gg, axis=0, keepdims=True)
@@ -233,8 +228,8 @@
             src_ref=zlo.at[to], dst_ref=lor.at[n], send_sem=sl.at[0], recv_sem=rl.at[0],
             device_id=(to, ex), device_id_type=MESH)
 
+    each(1, WINDOW + 1, lambda n, group: main_in(n, group).start())
     each(1, 32, lambda n, group: lo_in(n, group).start())
-    each(1, WINDOW + 1, lambda n, group: main_in(n, group).start())
     save_nm = pltpu.make_async_copy(nm, nm_hbm, nm_sem)
     save_nm.start()
     x[0:16, :] = zmain[pl.ds(pl.multiple_of(dp * 16, 16), 16), :]
@@ -268,9 +263,6 @@
         main_in(n, group).start()
     each(WINDOW + 1, GROUPS[0] + WINDOW, go)
 
-    def all_of(ref_at, sem, n=0):
-        pltpu.make_async_copy(ref_at, ref_at, sem.at[n]).wait()
-
     all_of(x.at[pl.ds(16, SHORT - 16)], rm, 0)
     all_of(lor.at[pl.ds(1, MATS - 1)], rl)
     x[SHORT:SHORT + 64, :] = lor[...].astype(F32).reshape(64, CDEV).astype(BF16)
@@ -494,7 +486,7 @@
             V(wide, BF16), V((MATS, 2, CDEV), BF16), V((MAIN, CDEV), BF16), V((MATS, 2, CDEV), BF16), V((64, CDEV), BF16),
             V(wide, BF16), V(wide, BF16),
             D((2, LOADS)), D, D, D((len(OUT_PARTS) + 1,)),
-            D((8,)), D((8,)), D((16,)), D((16,)), D((32,)), D((len(GROUPS),)), D((1,)), D((1,)),
+            D((8,)), D((1,)), D((16,)), D((1,)), D((32,)), D((len(GROUPS),)), D((1,)), D((1,)),
             D((len(OUT_PARTS),)), D((len(OUT_PARTS),)), D((1,)), D((1,)), D((18,)), D((18,)),
         ],
         compiler_params=pltpu.CompilerParams(collective_id=0, has_side_effects=True, vmem_limit_bytes=VMEM_LIMIT),

time: 109 us -> 108 us (level)
  no operation moved by 1% of the time
where the time goes in v6:
time: 108 us
  Pallas kernels  102 us (94%)
  local copies, waits for them, and re-layouts  5.9 us (5%)
    pallas_call x1, Pallas kernels, step(): pl.pallas_call(kernel, out_shape=(jax.ShapeDtypeStruct(wide, F32), jax.Sh...  102 us
    unnamed x7, local copies, waits for them, and re-layouts  5.9 us

profile of v6, /device:TPU:1, one launch (start us, length us, event | category | flops | bytes accessed | tf_op | source)
XLA Modules:
  0.0 108.2 jit_solution(12070075449371680522)
XLA Ops:
  0.6 0.0 copy-start
  0.6 0.6 copy-done
  1.3 0.0 copy-start.1
  1.3 0.7 copy-done.1
  1.9 101.7 %shard_map.67 = (f32[576,1792]{1,0:T(8,128)S(1)}, bf16[576,1792]{1,0:T(8,128)(2,1)S(1)}, bf16[576,1792]{1,0:T(8,128)(2,1)S(1)}) custom-call(s32[32]{0:T(128)S(1)} %copy-done, s32[32]{0:T(128)S(1)} %copy-done.1, f32[576,1792]{1,0:T(8,128)} %bitcast.16, f32[576,1792]{1,0:T(8,128)} %bitcast.17), custom_call_target="tpu_custom_call" | custom-call | tf_op jit(solution)/shard_map/pallas_call | solution.py:473
  103.6 2.0 %copy.10 = f32[32,18,1792]{2,0,1:T(8,128)} copy(f32[32,18,1792]{2,0,1:T(8,128)S(1)} %bitcast.13) | data formatting | bytes 8257536
  105.6 1.3 %copy.11 = bf16[32,18,1792]{2,0,1:T(8,128)(2,1)} copy(bf16[32,18,1792]{2,0,1:T(8,128)(2,1)S(1)} %bitcast.15) | data formatting | bytes 4128768
  106.9 1.3 %copy.12 = bf16[1,576,1792]{2,1,0:T(8,128)(2,1)} copy(bf16[1,576,1792]{2,1,0:T(8,128)(2,1)S(1)} %bitcast.14) | data formatting | bytes 4128768
Async XLA Ops:
  0.6 0.7 copy-start
  1.3 0.7 copy-start.1
